TPU v7x, 32 devices: a whole 2x2x4 slice. The times are simulated.
32 devices in a mesh: dp: 4 (over x, core), tok: 8 (over z, y).
Axes of the slice: x: 2, y: 2, z: 4, core: 2. Of those that a mesh axis runs over, the one named last changes fastest.
Arguments:
- tokens: bfloat16 [8, 1024, 768], P('dp', 'tok'), may hold values from -6 to 6
- mask: int32 [8, 1024], P('dp', 'tok'), may hold values 0 or 1
- segments: int32 [8, 1024], P('dp', 'tok'), may hold values from 0 to 3, as said below
- replacement: float32 [768], replicated, may hold values from -6 to 6
- w_qkv: bfloat16 [768, 2, 2304], replicated, may hold values from -0.21875 to 0.21875
- w_out: bfloat16 [768, 2, 768], replicated, may hold values from -0.875 to 0.875
- w_in: bfloat16 [768, 2, 6144], replicated, may hold values from -0.21875 to 0.21875
- w_down: bfloat16 [3072, 2, 768], replicated, may hold values from -0.109375 to 0.109375
- ln_gain: float32 [2, 2, 768], replicated, may hold values from 0.5 to 1.5
- ln_bias: float32 [2, 2, 768], replicated, may hold values from -1 to 1
- cotangent: bfloat16 [8, 1024, 768], P('dp', 'tok'), may hold values from -6 to 6
Outputs:
- layer_out: bfloat16 [8, 1024, 768], P('dp', 'tok')
- grad_tokens: float32 [8, 1024, 768], P('dp', 'tok')
- grad_replacement: float32 [768], P('tok')
- grad_w_qkv: float32 [768, 2, 2304], P('tok')
- grad_w_out: float32 [768, 2, 768], P('tok')
- grad_w_in: float32 [768, 2, 6144], P('tok')
- grad_w_down: float32 [3072, 2, 768], P('tok')
- grad_gain: float32 [2, 2, 768], P(None, None, 'tok')
- grad_bias: float32 [2, 2, 768], P(None, None, 'tok')
Inputs may be any that keep to these rules, and one draw needn't show every extreme that they name: `segments`: along each sequence the ids start at 0 and never fall. Each sequence holds either one document or exactly 4. In each aligned group of 2 sequences exactly one, at a place drawn from the seed, is a single document.
All inputs are finite; a program needn't handle non-finite values. No bound on the sum of `mask` on one device may be relied on, other than what follows from the above.
Results may differ from a plain program's by a relative error of at most 0.025.
Values may be sent and summed in bfloat16 or wider, within the bound.
No kernel may reach another device: no remote copies, remote signals or barrier semaphores. Data moves between devices by JAX's collectives and lax.ppermute only.
A program may use at most 384 MiB of HBM per device.

v0:
```python
import math

import jax
import jax.numpy as jnp
from jax import lax
from jax.sharding import PartitionSpec as P

HEADS = 12
HEAD_DIM = 64
LAYERS = 2


def alibi_slopes(head_count):
    head_index = jnp.arange(head_count, dtype=jnp.float32)
    return jnp.exp2(jnp.where(head_index < 8.0, -(head_index + 1.0), 7.5 - head_index))


def layer_norm(value, gain, bias):
    center = jnp.mean(value, axis=-1, keepdims=True)
    shifted = value - center
    spread = jnp.mean(shifted * shifted, axis=-1, keepdims=True)
    return shifted * lax.rsqrt(spread + 1e-12) * gain + bias


def gated_gelu(gate_up):
    half_cols = gate_up.shape[-1] // 2
    return jax.nn.gelu(gate_up[..., :half_cols], approximate=False) * gate_up[..., half_cols:]


def masked_scores(
    queries, key_rows, query_labels, key_labels, query_pos, key_pos, slopes, score_scale
):
    raw_scores = (
        jnp.einsum("qhc,khc->hqk", queries, key_rows, preferred_element_type=jnp.float32)
        * score_scale
    )
    distance = jnp.abs(query_pos[:, None] - key_pos[None, :]).astype(jnp.float32)
    scores = raw_scores - slopes[:, None, None] * distance[None]
    same_doc = query_labels[:, None] == key_labels[None, :]
    return jnp.where(same_doc[None], scores, -jnp.inf)


def scores_for(queries, key_rows, query_labels, labels_all, query_pos, slopes, score_scale):
    full_len = key_rows.shape[0]
    key_width = min(128, full_len)
    score_parts = []
    for key_first in range(0, full_len, key_width):
        block_keys = key_rows[key_first : key_first + key_width]
        block_labels = labels_all[key_first : key_first + key_width]
        block_pos = key_first + jnp.arange(key_width, dtype=jnp.int32)
        score_parts.append(
            masked_scores(
                queries,
                block_keys,
                query_labels,
                block_labels,
                query_pos,
                block_pos,
                slopes,
                score_scale,
            )
        )
    return jnp.concatenate(score_parts, axis=2)


def attend_forward(queries, key_rows, value_rows, labels, slopes, score_scale):
    unit_count, full_len, per_group, head_dim = queries.shape
    block_rows = min(512, full_len)
    block_count = full_len // block_rows

    def one_block(flat_index):
        unit_index = flat_index // block_count
        first_row = flat_index % block_count * block_rows
        unit_queries = lax.dynamic_index_in_dim(queries, unit_index, 0, False)
        unit_keys = lax.dynamic_index_in_dim(key_rows, unit_index, 0, False)
        unit_values = lax.dynamic_index_in_dim(value_rows, unit_index, 0, False)
        unit_labels = lax.dynamic_index_in_dim(labels, unit_index, 0, False)
        block_queries = lax.dynamic_slice_in_dim(unit_queries, first_row, block_rows, 0)
        block_labels = lax.dynamic_slice_in_dim(unit_labels, first_row, block_rows, 0)
        query_pos = first_row + jnp.arange(block_rows, dtype=jnp.int32)
        scores = scores_for(
            block_queries, unit_keys, block_labels, unit_labels, query_pos, slopes, score_scale
        )
        row_max = jnp.max(scores, axis=-1, keepdims=True)
        weights_exp = jnp.exp(scores - row_max)
        row_sum = jnp.sum(weights_exp, axis=-1, keepdims=True)
        probability = (weights_exp / row_sum).astype(jnp.bfloat16)
        context = jnp.einsum(
            "hqk,khc->qhc", probability, unit_values, preferred_element_type=jnp.float32
        )
        return (context, (row_max + jnp.log(row_sum))[..., 0])

    context, log_total = lax.map(one_block, jnp.arange(unit_count * block_count))
    return (
        context.reshape(unit_count, full_len, per_group, head_dim),
        log_total.reshape(unit_count, block_count, per_group, block_rows),
    )


def attend_backward(
    queries, key_rows, value_rows, context_grad, log_total, labels, slopes, score_scale
):
    unit_count, full_len, per_group, head_dim = queries.shape
    block_rows = min(512, full_len)
    block_count = full_len // block_rows

    def per_unit(unit_index):
        unit_queries = lax.dynamic_index_in_dim(queries, unit_index, 0, False)
        unit_keys = lax.dynamic_index_in_dim(key_rows, unit_index, 0, False)
        unit_values = lax.dynamic_index_in_dim(value_rows, unit_index, 0, False)
        unit_grads = lax.dynamic_index_in_dim(context_grad, unit_index, 0, False)
        unit_totals = lax.dynamic_index_in_dim(log_total, unit_index, 0, False)
        unit_labels = lax.dynamic_index_in_dim(labels, unit_index, 0, False)

        def one_step(carried, block_index):
            key_acc, value_acc = carried
            first_row = block_index * block_rows
            block_queries = lax.dynamic_slice_in_dim(unit_queries, first_row, block_rows, 0)
            block_grads = lax.dynamic_slice_in_dim(unit_grads, first_row, block_rows, 0)
            block_labels = lax.dynamic_slice_in_dim(unit_labels, first_row, block_rows, 0)
            block_totals = lax.dynamic_index_in_dim(unit_totals, block_index, 0, False)
            query_pos = first_row + jnp.arange(block_rows, dtype=jnp.int32)
            scores = scores_for(
                block_queries, unit_keys, block_labels, unit_labels, query_pos, slopes, score_scale
            )
            probability = jnp.exp(scores - block_totals[..., None])
            prob_grad = jnp.einsum(
                "qhc,khc->hqk", block_grads, unit_values, preferred_element_type=jnp.float32
            )
            inner = jnp.sum(probability * prob_grad, axis=-1, keepdims=True)
            score_grad = (probability * (prob_grad - inner)).astype(jnp.bfloat16)
            query_grad = (
                jnp.einsum(
                    "hqk,khc->qhc", score_grad, unit_keys, preferred_element_type=jnp.float32
                )
                * score_scale
            )
            key_acc = (
                key_acc
                + jnp.einsum(
                    "hqk,qhc->khc", score_grad, block_queries, preferred_element_type=jnp.float32
                )
                * score_scale
            )
            value_acc = value_acc + jnp.einsum(
                "hqk,qhc->khc",
                probability.astype(jnp.bfloat16),
                block_grads,
                preferred_element_type=jnp.float32,
            )
            return ((key_acc, value_acc), query_grad)

        zero_rows = jnp.zeros((full_len, per_group, head_dim), jnp.float32)
        (key_grad, value_grad), query_grad = lax.scan(
            one_step, (zero_rows, zero_rows), jnp.arange(block_count)
        )
        return (query_grad.reshape(full_len, per_group, head_dim), key_grad, value_grad)

    return lax.map(per_unit, jnp.arange(unit_count))


def per_device(
    tokens, mask, segments, replacement, w_qkv, w_out, w_in, w_down, ln_gain, ln_bias, cotangent
):
    group_count = 4
    tok_devices = lax.axis_size("tok")
    seq_count, local_len, model_width = tokens.shape
    row_groups = tok_devices // group_count
    unit_count = seq_count // row_groups
    per_group = HEADS // group_count
    group_cols = per_group * HEAD_DIM
    tok_count = seq_count * local_len
    full_len = local_len * tok_devices
    score_scale = 1.0 / math.sqrt(HEAD_DIM)
    tok_place = lax.axis_index("tok")
    head_group = tok_place // row_groups
    labels_all = lax.all_gather(segments, "tok", axis=1, tiled=True)
    labels_mine = lax.dynamic_slice_in_dim(
        labels_all, tok_place % row_groups * unit_count, unit_count, 0
    )
    slopes = lax.dynamic_slice_in_dim(alibi_slopes(HEADS), head_group * per_group, per_group, 0)
    masked = (mask == 1).reshape(tok_count, 1)
    current = jnp.where(
        masked, replacement[None, :], tokens.reshape(tok_count, model_width).astype(jnp.float32)
    )
    stored = []
    for layer_index in range(LAYERS):
        w_qkv_layer = w_qkv[:, layer_index].reshape(model_width, 3, group_count, group_cols)
        w_out_layer = w_out[:, layer_index].reshape(group_count, group_cols, model_width)
        flat_in = current.astype(jnp.bfloat16)
        projected = jnp.einsum(
            "nd,dkgc->gnkc", flat_in, w_qkv_layer, preferred_element_type=jnp.float32
        ).astype(jnp.bfloat16)
        projected = lax.all_to_all(
            projected.reshape(tok_devices, unit_count, local_len, 3 * group_cols),
            "tok",
            split_axis=0,
            concat_axis=2,
            tiled=True,
        )
        projected = projected.reshape(unit_count, full_len, 3, per_group, HEAD_DIM)
        queries = projected[:, :, 0]
        key_rows = projected[:, :, 1]
        value_rows = projected[:, :, 2]
        context, log_total = attend_forward(
            queries, key_rows, value_rows, labels_mine, slopes, score_scale
        )
        context = lax.all_to_all(
            context.astype(jnp.bfloat16).reshape(1, unit_count, full_len, group_cols),
            "tok",
            split_axis=2,
            concat_axis=0,
            tiled=True,
        )
        context = context.reshape(group_count, tok_count, group_cols)
        branch = jnp.einsum("gnc,gcd->nd", context, w_out_layer, preferred_element_type=jnp.float32)
        summed = current + branch
        normed_one = layer_norm(summed, ln_gain[layer_index, 0], ln_bias[layer_index, 0])
        normed_low = normed_one.astype(jnp.bfloat16)
        gate_up = jnp.dot(normed_low, w_in[:, layer_index], preferred_element_type=jnp.float32)
        hidden = gated_gelu(gate_up).astype(jnp.bfloat16)
        mixed_sum = normed_one + jnp.dot(
            hidden, w_down[:, layer_index], preferred_element_type=jnp.float32
        )
        stored.append(
            (
                flat_in,
                queries,
                key_rows,
                value_rows,
                log_total,
                context,
                summed,
                normed_low,
                gate_up,
                hidden,
                mixed_sum,
            )
        )
        current = layer_norm(mixed_sum, ln_gain[layer_index, 1], ln_bias[layer_index, 1])
    layer_out = current.reshape(seq_count, local_len, model_width).astype(jnp.bfloat16)
    gradient = cotangent.reshape(tok_count, model_width).astype(jnp.float32)
    grads_qkv = [None] * LAYERS
    grads_out = [None] * LAYERS
    grads_in = [None] * LAYERS
    grads_down = [None] * LAYERS
    grads_gain = [None] * LAYERS
    grads_bias = [None] * LAYERS
    for layer_index in reversed(range(LAYERS)):
        (
            flat_in,
            queries,
            key_rows,
            value_rows,
            log_total,
            context,
            summed,
            normed_low,
            gate_up,
            hidden,
            mixed_sum,
        ) = stored[layer_index]
        w_qkv_layer = w_qkv[:, layer_index].reshape(model_width, 3, group_count, group_cols)
        w_out_layer = w_out[:, layer_index].reshape(group_count, group_cols, model_width)
        w_in_layer = w_in[:, layer_index]
        w_down_layer = w_down[:, layer_index]
        norm_back = jax.vjp(
            layer_norm, mixed_sum, ln_gain[layer_index, 1], ln_bias[layer_index, 1]
        )[1]
        mixed_grad, gain_two, bias_two = norm_back(gradient)
        mixed_low = mixed_grad.astype(jnp.bfloat16)
        grads_down[layer_index] = jnp.einsum(
            "nf,nd->fd", hidden, mixed_low, preferred_element_type=jnp.float32
        )
        hidden_grad = jnp.einsum(
            "nd,fd->nf", mixed_low, w_down_layer, preferred_element_type=jnp.float32
        )
        gate_grad = jax.vjp(gated_gelu, gate_up)[1](hidden_grad)[0].astype(jnp.bfloat16)
        grads_in[layer_index] = jnp.einsum(
            "nd,ne->de", normed_low, gate_grad, preferred_element_type=jnp.float32
        )
        normed_grad = mixed_grad + jnp.einsum(
            "ne,de->nd", gate_grad, w_in_layer, preferred_element_type=jnp.float32
        )
        first_back = jax.vjp(layer_norm, summed, ln_gain[layer_index, 0], ln_bias[layer_index, 0])[
            1
        ]
        summed_grad, gain_one, bias_one = first_back(normed_grad)
        grads_gain[layer_index] = jnp.stack((gain_one, gain_two), axis=0)
        grads_bias[layer_index] = jnp.stack((bias_one, bias_two), axis=0)
        summed_low = summed_grad.astype(jnp.bfloat16)
        grads_out[layer_index] = jnp.einsum(
            "gnc,nd->gcd", context, summed_low, preferred_element_type=jnp.float32
        ).reshape(model_width, model_width)
        context_grad = jnp.einsum(
            "nd,gcd->gnc", summed_low, w_out_layer, preferred_element_type=jnp.float32
        ).astype(jnp.bfloat16)
        context_grad = lax.all_to_all(
            context_grad.reshape(tok_devices, unit_count, local_len, group_cols),
            "tok",
            split_axis=0,
            concat_axis=2,
            tiled=True,
        )
        context_grad = context_grad.reshape(unit_count, full_len, per_group, HEAD_DIM)
        query_grad, key_grad, value_grad = attend_backward(
            queries, key_rows, value_rows, context_grad, log_total, labels_mine, slopes, score_scale
        )
        head_grad = jnp.stack((query_grad, key_grad, value_grad), axis=2).astype(jnp.bfloat16)
        head_grad = lax.all_to_all(
            head_grad.reshape(1, unit_count, full_len, 3 * group_cols),
            "tok",
            split_axis=2,
            concat_axis=0,
            tiled=True,
        )
        head_grad = head_grad.reshape(group_count, tok_count, 3, group_cols)
        grads_qkv[layer_index] = jnp.einsum(
            "nd,gnkc->dkgc", flat_in, head_grad, preferred_element_type=jnp.float32
        ).reshape(model_width, 3 * model_width)
        gradient = summed_grad + jnp.einsum(
            "gnkc,dkgc->nd", head_grad, w_qkv_layer, preferred_element_type=jnp.float32
        )
    grad_tokens = jnp.where(masked, 0.0, gradient).reshape(seq_count, local_len, model_width)
    replacement_grad = jnp.sum(jnp.where(masked, gradient, 0.0), axis=0)
    members = (
        jnp.stack(grads_qkv, axis=1),
        jnp.stack(grads_out, axis=1),
        jnp.stack(grads_in, axis=1),
        jnp.stack(grads_down, axis=1),
        jnp.stack(grads_gain, axis=0),
        jnp.stack(grads_bias, axis=0),
        replacement_grad,
    )
    shares = (
        lax.psum_scatter(
            members[0].astype(jnp.bfloat16), "tok", scatter_dimension=0, tiled=True
        ).astype(jnp.float32),
        lax.psum_scatter(
            members[1].astype(jnp.bfloat16), "tok", scatter_dimension=0, tiled=True
        ).astype(jnp.float32),
        lax.psum_scatter(
            members[2].astype(jnp.bfloat16), "tok", scatter_dimension=0, tiled=True
        ).astype(jnp.float32),
        lax.psum_scatter(
            members[3].astype(jnp.bfloat16), "tok", scatter_dimension=0, tiled=True
        ).astype(jnp.float32),
        lax.psum_scatter(
            members[4].astype(jnp.bfloat16), "tok", scatter_dimension=2, tiled=True
        ).astype(jnp.float32),
        lax.psum_scatter(
            members[5].astype(jnp.bfloat16), "tok", scatter_dimension=2, tiled=True
        ).astype(jnp.float32),
        lax.psum_scatter(
            members[6].astype(jnp.bfloat16), "tok", scatter_dimension=0, tiled=True
        ).astype(jnp.float32),
    )
    totals = (
        lax.psum(shares[0].astype(jnp.bfloat16), "dp").astype(jnp.float32),
        lax.psum(shares[1].astype(jnp.bfloat16), "dp").astype(jnp.float32),
        lax.psum(shares[2].astype(jnp.bfloat16), "dp").astype(jnp.float32),
        lax.psum(shares[3].astype(jnp.bfloat16), "dp").astype(jnp.float32),
        lax.psum(shares[4].astype(jnp.bfloat16), "dp").astype(jnp.float32),
        lax.psum(shares[5].astype(jnp.bfloat16), "dp").astype(jnp.float32),
        lax.psum(shares[6].astype(jnp.bfloat16), "dp").astype(jnp.float32),
    )
    return (
        layer_out,
        grad_tokens,
        totals[6],
        totals[0],
        totals[1],
        totals[2],
        totals[3],
        totals[4],
        totals[5],
    )


def solution(mesh):
    in_specs = (
        P("dp", "tok", None),
        P("dp", "tok"),
        P("dp", "tok"),
        P(),
        P(),
        P(),
        P(),
        P(),
        P(),
        P(),
        P("dp", "tok", None),
    )
    out_specs = (
        P("dp", "tok", None),
        P("dp", "tok", None),
        P("tok"),
        P("tok", None, None),
        P("tok", None, None),
        P("tok", None, None),
        P("tok", None, None),
        P(None, None, "tok"),
        P(None, None, "tok"),
    )
    return jax.shard_map(
        per_device, mesh=mesh, in_specs=in_specs, out_specs=out_specs, check_vma=False
    )
```

profile of v0, /device:TPU:0, one launch (start us, length us, event | category | flops | bytes accessed | tf_op | source)
XLA Modules:
  0.0 1843.9 jit_solution(1345929105138833218)
XLA Ops:
  7.2 15.2 fusion.373
  22.4 16.0 copy.193
  51.2 34.1 %all_gather.3 = s32[2,1024]{1,0:T(2,128)S(1)} all-gather(s32[2,128]{1,0:T(2,128)S(1)} %copy-done.125), channel_id=1, replica_groups=mesh['dp'=4,'tok'=8] {'tok'}, dimensions={1}, use_global_device_ids=true | all-gather | bytes 9216 | tf_op jit(solution)/shard_map/all_gather | solution.py:177
  85.2 36.7 %fusion.371 = (bf16[768,1,6144]{2,1,0:T(2,128)(2,1)}, bf16[768,1,6144]{2,1,0:T(2,128)(2,1)}) fusion(bf16[768,2,6144]{2,1,0:T(2,128)(2,1)} %param.25), kind=kLoop, calls=%fused_computation.657 | loop fusion | bytes 37748736 | tf_op jit(solution)/shard_map/slice | solution.py:220
  122.6 19.2 %fusion.372 = (bf16[3072,1,768]{2,1,0:T(2,128)(2,1)}, bf16[3072,1,768]{2,1,0:T(2,128)(2,1)}) fusion(bf16[3072,2,768]{2,1,0:T(2,128)(2,1)} %param.26), kind=kLoop, calls=%fused_computation.658 | loop fusion | bytes 18874368 | tf_op jit(solution)/shard_map/slice | solution.py:223
  144.5 32.7 %while.80 = (s32[]{:T(128)}, bf16[2,512,3,64]{1,3,2,0:T(8,128)(2,1)S(1)}, f32[2,3,512]{2,1,0:T(4,128)S(1)}, s32[2]{0:T(128)S(1)}, s32[1,1024]{1,0:T(1,128)S(1)},...) while((s32[]{:T(128)}, ...), condition=%wide.region_10.11_spmd, body=%wide.region_0.10_spmd.sunk | while | flops 420478848 | bytes 27077980 | solution.py:93
  200.5 16.3 copy.204
  253.2 25.5 %all-to-all-done.2 = bf16[8,1,128,576]{2,3,1,0:T(8,128)(2,1)S(1)} async-done(((bf16[8,1,128,576]{2,3,1,0:T(8,128)(2,1)}), bf16[8,1,128,576]{2,3,1,0:T(8,128)(2,1)S(1)}, u32[]{:S(2)}, u32[]{:S(2)}) %all-to-all-start.2) | async-done | bytes 1179680 | tf_op jit(solution)/shard_map/all_to_all | solution.py:194
  283.2 36.0 %while.81 = (s32[]{:T(128)}, bf16[2,512,3,64]{1,3,2,0:T(8,128)(2,1)}, f32[2,3,512]{2,1,0:T(4,128)}, s32[2]{0:T(128)}, s32[1,1024]{1,0:T(1,128)S(1)}, /*index=5*/...) while((s32[]{:T(128)}, ...), condition=%wide.region_25.26_spmd, body=%wide.region_15.25_spmd.sunk | while | flops 420478848 | bytes 31895016 | solution.py:93
  382.2 17.4 multiply_reduce_fusion.2
  419.9 78.3 %while.82 = (s32[]{:T(128)}, f32[1024,3,64]{0,2,1:T(8,128)}, f32[1024,3,64]{0,2,1:T(8,128)}, bf16[2,512,3,64]{1,3,2,0:T(8,128)(2,1)}, s32[2]{0:T(128)}, /*index=...) while((s32[]{:T(128)}, f32[1024,3,64]{0,2,1:T(8,128)}, ...), condition=%wide.region_36.37_spmd.clone, body=%wide.region_34.36_spmd.clone.sunk | while | flops 1030258560 | bytes 70448664 | solution.py:154
  521.2 32.4 %all_to_all.32 = bf16[8,2,36864]{2,1,0:T(2,128)(2,1)} all-to-all(bf16[8,2,36864]{2,1,0:T(2,128)(2,1)S(1)} %reshape.2865), channel_id=1, replica_groups=mesh['dp'=4,'tok'=8] {'tok'}, dimensions={0} | all-to-all | bytes 2359296 | tf_op jit(solution)/shard_map/all_to_all | solution.py:310
  589.3 17.0 multiply_reduce_fusion.4
  625.9 77.7 %while.83 = (s32[]{:T(128)}, f32[1024,3,64]{0,2,1:T(8,128)}, f32[1024,3,64]{0,2,1:T(8,128)}, bf16[2,512,3,64]{1,3,2,0:T(8,128)(2,1)}, s32[2]{0:T(128)}, /*index=...) while((s32[]{:T(128)}, f32[1024,3,64]{0,2,1:T(8,128)}, ...), condition=%wide.region_43.44_spmd.clone, body=%wide.region_41.43_spmd.clone.sunk | while | flops 1030258560 | bytes 68875776 | solution.py:154
  733.6 26.2 %all-to-all-done.7 = bf16[8,2,36864]{2,1,0:T(2,128)(2,1)} async-done(((bf16[8,2,36864]{2,1,0:T(2,128)(2,1)}), bf16[8,2,36864]{2,1,0:T(2,128)(2,1)}, u32[]{:S(2)}, u32[]{:S(2)}) %all-to-all-start.7) | async-done | bytes 1179680 | tf_op jit(solution)/shard_map/all_to_all | solution.py:310
  792.2 18.2 copy.235
  866.1 177.1 %all-reduce.11.cloned.1.call-done = bf16[768,2,2304]{2,1,0:T(2,128)(2,1)} async-done(((bf16[768,2,2304]{2,1,0:T(2,128)(2,1)}), bf16[768,2,2304]{2,1,0:T(2,128)(2,1)}) %all-reduce.11.cloned.1.call-update) | async-done | bytes 7077904
  1046.0 70.1 %reduce-scatter.10.cloned.1.call-done = bf16[96,2,768]{2,0,1:T(8,128)(2,1)} async-done(((bf16[768,2,768]{2,0,1:T(8,128)(2,1)}), bf16[96,2,768]{2,0,1:T(8,128)(2,1)}) %reduce-scatter.10.cloned.1.call-update) | async-done | bytes 294928 | tf_op jit(solution)/shard_map/reduce_scatter | solution.py:339
  1116.0 166.5 %reduce-scatter.14.cloned.1.call-done = bf16[384,2,768]{2,0,1:T(8,128)(2,1)} async-done(((bf16[3072,2,768]{2,0,1:T(8,128)(2,1)}), bf16[384,2,768]{2,0,1:T(8,128)(2,1)}) %reduce-scatter.14.cloned.1.call-update) | async-done | bytes 1179664 | tf_op jit(solution)/shard_map/reduce_scatter | solution.py:345
  1282.6 316.7 %reduce-scatter.12.cloned.1.call-done = bf16[96,2,6144]{2,0,1:T(8,128)(2,1)} async-done(((bf16[768,2,6144]{2,0,1:T(8,128)(2,1)}), bf16[96,2,6144]{2,0,1:T(8,128)(2,1)}) %reduce-scatter.12.cloned.1.call-update) | async-done | bytes 2359312 | tf_op jit(solution)/shard_map/reduce_scatter | solution.py:342
  1599.3 64.3 %reduce-scatter.18.cloned.1.call-done = bf16[96,4]{1,0:T(8,128)(2,1)} async-done(((bf16[768,4]{1,0:T(8,128)(2,1)}), bf16[96,4]{1,0:T(8,128)(2,1)}) %reduce-scatter.18.cloned.1.call-update) | async-done | bytes 784
  1664.5 63.3 %reduce-scatter.16.cloned.1.call-done = bf16[96,4]{1,0:T(8,128)(2,1)} async-done(((bf16[768,4]{1,0:T(8,128)(2,1)}), bf16[96,4]{1,0:T(8,128)(2,1)}) %reduce-scatter.16.cloned.1.call-update) | async-done | bytes 784
  1732.7 19.5 %all-reduce.4 = bf16[768]{0:T(1024)(128)(2,1)S(1)} all-reduce(bf16[768]{0:T(1024)(128)(2,1)S(1)} %get-tuple-element.869), channel_id=2, replica_groups=mesh['dp'=4,'tok'=8] {'tok'}, use_global_device_ids=true, to_apply=%region_45.46.clone | all-reduce | flops 768 | bytes 3072
  1760.4 64.4 %all-reduce.13.cloned.1.call-done = (bf16[96,2,768]{2,0,1:T(8,128)(2,1)}, bf16[96,2,6144]{2,0,1:T(8,128)(2,1)}, bf16[384,2,768]{2,0,1:T(8,128)(2,1)}, bf16[96,2,2304]{2,1,0:T(2,128)(2,1)}) async-done(((bf16[96,2,768]{2,0,1:T(8,128)(2,1)}, bf16[96,2,6144]{2,0,1:T(8,128)(2,1)}, bf16[384,2,768]{2,0,1:T(8,128)(2,1)}, bf16[96,2,2304]{2,1,0:T(2,128)(2,1)}), (bf16[96,2,768]{2,0,1:T(8,128)(2,1)}, ...) | async-done | bytes 4718608 | tf_op jit(solution)/shard_map/psum | solution.py:360
  (707 shorter events, 592.8 us)
Async XLA Ops:
  43.9 97.9 %all-to-all-start = ((bf16[8,1,128,576]{2,3,1,0:T(8,128)(2,1)}), bf16[8,1,128,576]{2,3,1,0:T(8,128)(2,1)S(1)}, u32[]{:S(2)}, u32[]{:S(2)}) async-start(bf16[8,1,128,576]{2,3,1,0:T(8,128)(2,1)} %copy.195), calls=%async_computation | async-start | bytes 2359296 | tf_op jit(solution)/shard_map/all_to_all | solution.py:194
  189.3 28.4 %all-to-all-start.1 = ((bf16[8,2,12288]{2,1,0:T(2,128)(2,1)}), bf16[8,2,12288]{2,1,0:T(2,128)(2,1)S(1)}, u32[]{:S(2)}, u32[]{:S(2)}) async-start(bf16[8,2,12288]{2,1,0:T(2,128)(2,1)} %reshape.2861), calls=%async_computation.1 | async-start | bytes 786432 | tf_op jit(solution)/shard_map/all_to_all | solution.py:208
  217.4 23.2 %copy-start.68 = (f32[768]{0:T(1024)}, f32[768]{0:T(1024)S(1)}, u32[]{:S(2)}) copy-start(f32[768]{0:T(1024)S(1)} %get-tuple-element.883) | copy-start | bytes 9220
  217.4 23.2 %copy-start.72 = (f32[768]{0:T(1024)}, f32[768]{0:T(1024)S(1)}, u32[]{:S(2)}) copy-start(f32[768]{0:T(1024)S(1)} %get-tuple-element.583) | copy-start | bytes 9220
  217.4 25.1 %copy-start.85 = (f32[768]{0:T(1024)}, f32[768]{0:T(1024)S(1)}, u32[]{:S(2)}) copy-start(f32[768]{0:T(1024)S(1)} %get-tuple-element.582) | copy-start | bytes 9220
  217.4 154.1 %copy-start.74 = (f32[768]{0:T(1024)}, f32[768]{0:T(1024)S(1)}, u32[]{:S(2)}) copy-start(f32[768]{0:T(1024)S(1)} %get-tuple-element.584) | copy-start | bytes 9220
  217.4 182.2 %copy-start.70 = (f32[768]{0:T(1024)}, f32[768]{0:T(1024)S(1)}, u32[]{:S(2)}) copy-start(f32[768]{0:T(1024)S(1)} %get-tuple-element.882) | copy-start | bytes 9220
  217.4 360.2 %copy-start.76 = (f32[768]{0:T(1024)}, f32[768]{0:T(1024)S(1)}, u32[]{:S(2)}) copy-start(f32[768]{0:T(1024)S(1)} %get-tuple-element.884) | copy-start | bytes 9220
  247.2 31.5 %all-to-all-start.2 = ((bf16[8,1,128,576]{2,3,1,0:T(8,128)(2,1)}), bf16[8,1,128,576]{2,3,1,0:T(8,128)(2,1)S(1)}, u32[]{:S(2)}, u32[]{:S(2)}) async-start(bf16[8,1,128,576]{2,3,1,0:T(8,128)(2,1)} %copy.206), calls=%async_computation.2 | async-start | bytes 2359296 | tf_op jit(solution)/shard_map/all_to_all | solution.py:194
  333.4 14.0 all-to-all-start.3
  351.1 48.6 %copy-start.24 = (f32[256,768]{1,0:T(8,128)}, f32[256,768]{1,0:T(8,128)S(1)}, u32[]{:S(2)}) copy-start(f32[256,768]{1,0:T(8,128)S(1)} %get-tuple-element.876) | copy-start | bytes 2359300
  403.4 14.7 all-to-all-start.4
  609.5 14.6 all-to-all-start.6
  727.8 32.0 %all-to-all-start.7 = ((bf16[8,2,36864]{2,1,0:T(2,128)(2,1)}), bf16[8,2,36864]{2,1,0:T(2,128)(2,1)}, u32[]{:S(2)}, u32[]{:S(2)}) async-start(bf16[8,2,36864]{2,1,0:T(2,128)(2,1)} %reshape.2867), calls=%async_computation.7 | async-start | bytes 2359296 | tf_op jit(solution)/shard_map/all_to_all | solution.py:310
  732.1 311.2 %all-reduce.11.cloned.1.call-start = ((), (), s32[]{:S(2)}) async-start(), calls=%async_computation.18 | async-start | bytes 14155776
  810.5 305.5 %reduce-scatter.10.cloned.1.call-start = ((), (), s32[]{:S(2)}) async-start(), calls=%async_computation.13 | async-start | bytes 2654208 | tf_op jit(solution)/shard_map/reduce_scatter | solution.py:339
  814.6 467.9 %reduce-scatter.14.cloned.1.call-start = ((), (), s32[]{:S(2)}) async-start(), calls=%async_computation.15 | async-start | bytes 10616832 | tf_op jit(solution)/shard_map/reduce_scatter | solution.py:345
  832.3 767.0 %reduce-scatter.12.cloned.1.call-start = ((), (), s32[]{:S(2)}) async-start(), calls=%async_computation.14 | async-start | bytes 21233664 | tf_op jit(solution)/shard_map/reduce_scatter | solution.py:342
  860.5 803.0 %reduce-scatter.18.cloned.1.call-start = ((), (), s32[]{:S(2)}) async-start(), calls=%async_computation.17 | async-start | bytes 221184
  864.4 863.3 %reduce-scatter.16.cloned.1.call-start = ((), (), s32[]{:S(2)}) async-start(), calls=%async_computation.16 | async-start | bytes 221184
  865.8 862.8 %copy-start.34 = (f32[256,768]{1,0:T(8,128)S(1)}, f32[256,768]{1,0:T(8,128)}, u32[]{:S(2)}) copy-start(f32[256,768]{1,0:T(8,128)} %copy-done.32) | copy-start | bytes 2359300
  865.8 862.8 %copy-start.38 = (bf16[4,256,3,192]{1,3,2,0:T(8,128)(2,1)S(1)}, bf16[4,256,3,192]{1,3,2,0:T(8,128)(2,1)}, u32[]{:S(2)}) copy-start(bf16[4,256,3,192]{1,3,2,0:T(8,128)(2,1)} %copy.229) | copy-start | bytes 3538948
  865.8 862.8 %copy-start.127 = (pred[256]{0:T(512)(128)(4,1)S(1)}, pred[256]{0:T(512)(128)(4,1)}, u32[]{:S(2)}) copy-start(pred[256]{0:T(512)(128)(4,1)} %copy-done.126) | copy-start | bytes 772
  865.8 959.0 %all-reduce.13.cloned.1.call-start = ((), (), s32[]{:S(2)}) async-start(), calls=%async_computation.19 | async-start | bytes 9437184 | tf_op jit(solution)/shard_map/psum | solution.py:360
  (147 other events, 1128.4 us)
Sparse Core Ops, SparseCore 0:
  810.6 232.6 all-reduce.10
  1047.7 68.2 reduce-scatter.9
  1120.0 162.4 reduce-scatter.13
  1286.8 312.4 reduce-scatter.11
  1603.3 60.2 reduce-scatter.17
  1667.6 60.0 reduce-scatter.15
  1731.1 93.7 all-reduce.12
where the time goes:
time: 1850 us; the launch traced here: 1840 us
  waiting for transfers between devices  1000 us (54%)
  matrix products  290 us (16%)
  local copies, waits for them, and re-layouts  271 us (15%)
  other arithmetic  115 us (6%)
  blocking collectives  92.5 us (5%)
  starting transfers between devices  35.8 us (2%)
    reduce_scatter x1, waiting for transfers between devices, per_device(): lax.psum_scatter(members[2].astype(jnp.bfloat16), 'tok', scatter_dimensio...  317 us
    unnamed x10, waiting for transfers between devices  305 us
    reduce_scatter x1, waiting for transfers between devices, per_device(): lax.psum_scatter(members[3].astype(jnp.bfloat16), 'tok', scatter_dimensio...  167 us
    dot_general x64, matrix products, masked_scores(): jnp.einsum('qhc,khc->hqk', queries, key_rows, preferred_element_type=jnp....  104 us
    reduce_scatter x1, waiting for transfers between devices, per_device(): lax.psum_scatter(members[1].astype(jnp.bfloat16), 'tok', scatter_dimensio...  70.1 us
    psum x1, waiting for transfers between devices, per_device(): lax.psum(shares[1].astype(jnp.bfloat16), 'dp').astype(jnp.float32)  64.4 us
    unnamed x259, local copies, waits for them, and re-layouts  50.6 us
    slice x3, local copies, waits for them, and re-layouts, per_device(): w_qkv[:, layer_index].reshape(model_width, 3, group_count, group_cols)  47.5 us
  transfers between devices with their start and end apart: 14, of which 12 were waited for; matrix products, arithmetic and copies ran while one was open for 8% of the time, Pallas kernels for 0%

commit v1 on v0

v1 whole, which is shorter than its diff:
```python
import math

import jax
import jax.numpy as jnp
from jax import lax
from jax.experimental import pallas as pl
from jax.experimental.pallas import tpu as pltpu
from jax.sharding import PartitionSpec as P

HEADS = 12
HEAD_DIM = 64
LAYERS = 2
LANES = 128
SCALE = 1.0 / math.sqrt(HEAD_DIM)
FAR = 1e30
BF16 = jnp.bfloat16
F32 = jnp.float32
VMEM_LIMIT = 56 << 20


def alibi_slopes(head_count):
    head_index = jnp.arange(head_count, dtype=jnp.float32)
    return jnp.exp2(jnp.where(head_index < 8.0, -(head_index + 1.0), 7.5 - head_index))


def layer_norm(value, gain, bias):
    center = jnp.mean(value, axis=-1, keepdims=True)
    shifted = value - center
    spread = jnp.mean(shifted * shifted, axis=-1, keepdims=True)
    return shifted * lax.rsqrt(spread + 1e-12) * gain + bias


def gated_gelu(gate_up):
    half_cols = gate_up.shape[-1] // 2
    return jax.nn.gelu(gate_up[..., :half_cols], approximate=False) * gate_up[..., half_cols:]


def dot(a, b, dims):
    return lax.dot_general(a, b, (dims, ((), ())), preferred_element_type=F32)


NN = ((1,), (0,))
NT = ((1,), (1,))
TN = ((0,), (0,))


def split_layers(weight):
    rows, _, cols = weight.shape
    row_block = 256
    col_block = next(c for c in (3072, 2304, 1152, 768) if cols % c == 0)

    def body(in_ref, out_ref):
        to_row = lax.broadcasted_iota(jnp.int32, (256, 256), 0)
        from_row = lax.broadcasted_iota(jnp.int32, (256, 256), 1)
        wanted = jnp.where(to_row < 128, 2 * to_row, 2 * to_row - 255)
        pick = jnp.where(from_row == wanted, 1.0, 0.0).astype(BF16)
        for part in range(row_block // 128):
            at = slice(part * 128, part * 128 + 128)
            mixed = in_ref[at].reshape(256, col_block)
            picked = dot(pick, mixed, NN).astype(BF16)
            out_ref[0, at] = picked[:128]
            out_ref[1, at] = picked[128:]

    return pl.pallas_call(
        body,
        grid=(rows // row_block, cols // col_block),
        in_specs=[pl.BlockSpec((row_block, 2, col_block), lambda i, j: (i, 0, j))],
        out_specs=pl.BlockSpec((2, row_block, col_block), lambda i, j: (0, i, j)),
        out_shape=jax.ShapeDtypeStruct((2, rows, cols), BF16),
        compiler_params=pltpu.CompilerParams(vmem_limit_bytes=VMEM_LIMIT),
        cost_estimate=pl.CostEstimate(
            flops=2 * 512 * rows * cols, bytes_accessed=8 * rows * cols, transcendentals=0
        ),
        name="split_layers",
    )(weight)


def attend_forward(qkv, far_dist, slopes):
    length, width = qkv.shape
    cols = width // 3
    heads = cols // HEAD_DIM
    block = 256

    def body(slope_ref, qkv_ref, dist_ref, ctx_ref, lse_ref):
        at = pl.ds(pl.multiple_of(pl.program_id(0) * block, block), block)
        dist = dist_ref[...]
        for h in range(heads):
            q = qkv_ref[at, h * 64 : h * 64 + 64]
            k = qkv_ref[:, cols + h * 64 : cols + h * 64 + 64]
            v = qkv_ref[:, 2 * cols + h * 64 : 2 * cols + h * 64 + 64]
            s = dot(k, q, NT) * SCALE - dist * slope_ref[h]
            top = jnp.max(s, axis=0, keepdims=True)
            e = jnp.exp(s - top)
            total = jnp.sum(e, axis=0, keepdims=True)
            ctx = dot(v, e.astype(BF16), TN) / total
            ctx_ref[:, h * 64 : h * 64 + 64] = ctx.T.astype(BF16)
            lse_ref[h : h + 1, :] = top + jnp.log(total)

    return pl.pallas_call(
        body,
        grid=(length // block,),
        in_specs=[
            pl.BlockSpec(memory_space=pltpu.SMEM),
            pl.BlockSpec((length, width), lambda i: (0, 0)),
            pl.BlockSpec((length, block), lambda i: (0, i)),
        ],
        out_specs=[
            pl.BlockSpec((block, cols), lambda i: (i, 0)),
            pl.BlockSpec((heads, block), lambda i: (0, i)),
        ],
        out_shape=[
            jax.ShapeDtypeStruct((length, cols), BF16),
            jax.ShapeDtypeStruct((heads, length), F32),
        ],
        compiler_params=pltpu.CompilerParams(vmem_limit_bytes=VMEM_LIMIT),
        cost_estimate=pl.CostEstimate(
            flops=16 * heads * length * length * HEAD_DIM,
            bytes_accessed=4 * length * length,
            transcendentals=heads * length * length,
        ),
        name="attend_forward",
    )(slopes, qkv, far_dist)


def attend_backward(qkv, ctx, ctx_grad, lse, far_dist, slopes):
    length, width = qkv.shape
    cols = width // 3
    heads = cols // HEAD_DIM
    block = 256

    def body(slope_ref, qkv_ref, ctx_ref, g_ref, lse_ref, dist_ref, out_ref, dk_ref, dv_ref):
        step = pl.program_id(0)
        at = pl.ds(pl.multiple_of(step * block, block), block)

        @pl.when(step == 0)
        def _():
            dk_ref[...] = jnp.zeros_like(dk_ref)
            dv_ref[...] = jnp.zeros_like(dv_ref)

        dist = dist_ref[...]
        for h in range(heads):
            mine = slice(h * 64, h * 64 + 64)
            q = qkv_ref[at, mine]
            k = qkv_ref[:, cols + h * 64 : cols + h * 64 + 64]
            v = qkv_ref[:, 2 * cols + h * 64 : 2 * cols + h * 64 + 64]
            g = g_ref[:, mine]
            inner = (g.astype(F32) * ctx_ref[:, mine].astype(F32)).T
            inner = jnp.sum(inner, axis=0, keepdims=True)
            s = dot(k, q, NT) * SCALE - dist * slope_ref[h]
            p = jnp.exp(s - lse_ref[h : h + 1, :])
            gp = dot(v, g, NT)
            gs = (p * (gp - inner)).astype(BF16)
            dv_ref[:, mine] += dot(p.astype(BF16), g, NN)
            dk_ref[:, mine] += dot(gs, q, NN)
            dq = dot(k, gs, TN) * SCALE
            out_ref[at, mine] = dq.T.astype(BF16)

        @pl.when(step == pl.num_programs(0) - 1)
        def _():
            out_ref[:, cols : 2 * cols] = (dk_ref[...] * SCALE).astype(BF16)
            out_ref[:, 2 * cols :] = dv_ref[...].astype(BF16)

    return pl.pallas_call(
        body,
        grid=(length // block,),
        in_specs=[
            pl.BlockSpec(memory_space=pltpu.SMEM),
            pl.BlockSpec((length, width), lambda i: (0, 0)),
            pl.BlockSpec((block, cols), lambda i: (i, 0)),
            pl.BlockSpec((block, cols), lambda i: (i, 0)),
            pl.BlockSpec((heads, block), lambda i: (0, i)),
            pl.BlockSpec((length, block), lambda i: (0, i)),
        ],
        out_specs=pl.BlockSpec((length, width), lambda i: (0, 0)),
        out_shape=jax.ShapeDtypeStruct((length, width), BF16),
        scratch_shapes=[pltpu.VMEM((length, cols), F32), pltpu.VMEM((length, cols), F32)],
        compiler_params=pltpu.CompilerParams(vmem_limit_bytes=VMEM_LIMIT),
        cost_estimate=pl.CostEstimate(
            flops=40 * heads * length * length * HEAD_DIM,
            bytes_accessed=4 * length * length,
            transcendentals=heads * length * length,
        ),
        name="attend_backward",
    )(slopes, qkv, ctx, ctx_grad, lse, far_dist)


def swap(value, axis, bit):
    return lax.ppermute(value, axis, [(i, i ^ (1 << bit)) for i in range(lax.axis_size(axis))])


def reduce_half(value, axis, bit, dim):
    mine = (lax.axis_index(axis) >> bit) & 1
    kept = lax.dynamic_index_in_dim(value, mine, dim, False)
    sent = lax.dynamic_index_in_dim(value, 1 - mine, dim, False)
    return (kept.astype(F32) + swap(sent, axis, bit).astype(F32)).astype(BF16)


def gather_pair(value, axis, bit, dim):
    mine = (lax.axis_index(axis) >> bit) & 1
    other = swap(value, axis, bit)
    low = jnp.where(mine == 0, value, other)
    high = jnp.where(mine == 0, other, value)
    return jnp.stack((low, high), axis=dim)


def bits_of(axis):
    return lax.axis_size(axis).bit_length() - 1


def reduce_tok(value):
    for bit in range(bits_of("tok")):
        count = value.shape[0]
        value = value.reshape(count // 2, 2, *value.shape[1:])
        value = reduce_half(value, "tok", bit, 1)
    return value[0]


def gather_dp(value):
    value = value[None]
    for bit in reversed(range(bits_of("dp"))):
        value = gather_pair(value, "dp", bit, 1)
        value = value.reshape(-1, *value.shape[2:])
    return value


def per_device(
    tokens, mask, segments, replacement, w_qkv, w_out, w_in, w_down, ln_gain, ln_bias, cotangent
):
    tok_devices = lax.axis_size("tok")
    dp_devices = lax.axis_size("dp")
    seq_count, local_len, width = tokens.shape
    sub = tok_devices // seq_count
    per_group = HEADS // sub
    cols = per_group * HEAD_DIM
    tok_count = seq_count * local_len
    full_len = local_len * tok_devices
    tok_place = lax.axis_index("tok")
    group = tok_place % sub
    apart = [[j + sub * k for k in range(seq_count)] for j in range(sub)]
    near = [[j + sub * k for j in range(sub)] for k in range(seq_count)]

    def regroup(value):
        return lax.all_to_all(value, "tok", 0, 0, axis_index_groups=apart)

    def spread(value):
        return lax.all_to_all(value, "tok", 0, 0, axis_index_groups=near)

    extra = jnp.zeros((seq_count, local_len, LANES), BF16)
    extra = extra.at[:, :, 0].set((mask == 1).astype(BF16))
    extra = extra.at[:, :, 1].set(segments.astype(BF16))
    mixed = regroup(jnp.concatenate((tokens, extra), axis=-1)).reshape(tok_count, -1)
    flags = mixed[:, width:]
    masked = flags[:, :1] == 1.0
    current = jnp.where(masked, replacement[None, :], mixed[:, :width].astype(F32))
    cot = regroup(cotangent).reshape(tok_count, width)

    wq = split_layers(w_qkv)
    wo = split_layers(w_out)
    wi = split_layers(w_in)
    wd = split_layers(w_down)
    wq_mine = lax.dynamic_index_in_dim(
        wq.reshape(LAYERS, width, 3, sub, cols), group, 3, False
    ).reshape(LAYERS, width, 3 * cols)
    slopes = lax.dynamic_slice_in_dim(alibi_slopes(HEADS), group * per_group, per_group, 0)
    place = jnp.arange(full_len, dtype=jnp.int32)
    place = place.reshape(seq_count, sub, local_len).transpose(1, 0, 2).reshape(full_len)
    far_dist = None
    stored = []
    for layer in range(LAYERS):
        flat_in = current.astype(BF16)
        sent = jnp.concatenate((flat_in, flags), axis=-1) if layer == 0 else flat_in
        flat_all = spread(jnp.broadcast_to(sent[None], (sub, *sent.shape)))
        flat_all = flat_all.reshape(full_len, -1)
        if layer == 0:
            labels = flat_all[:, width + 1].astype(F32)
            flat_all = flat_all[:, :width]
            far_dist = jnp.where(
                labels[:, None] == labels[None, :],
                jnp.abs(place[:, None] - place[None, :]).astype(F32),
                FAR,
            )
        qkv = dot(flat_all, wq_mine[layer], NN).astype(BF16)
        ctx_here, lse = attend_forward(qkv, far_dist, slopes)
        ctx = spread(ctx_here.reshape(sub, tok_count, cols))
        ctx = ctx.transpose(1, 0, 2).reshape(tok_count, width)
        summed = current + dot(ctx, wo[layer], NN)
        y1 = layer_norm(summed, ln_gain[layer, 0], ln_bias[layer, 0])
        y1l = y1.astype(BF16)
        gate_up = dot(y1l, wi[layer], NN)
        hidden = gated_gelu(gate_up).astype(BF16)
        z = y1 + dot(hidden, wd[layer], NN)
        lhs_all = lax.all_gather(jnp.concatenate((y1l, hidden), axis=-1), "dp", tiled=True)
        stored.append((flat_all, qkv, ctx_here, lse, ctx, summed, gate_up, z, lhs_all))
        current = layer_norm(z, ln_gain[layer, 1], ln_bias[layer, 1])
    layer_out = regroup(current.astype(BF16).reshape(seq_count, local_len, width))
    gradient = cot.astype(F32)
    outs = [None] * LAYERS
    small = []
    in_cols = wi.shape[2] // dp_devices
    down_cols = width // dp_devices
    ff = wd.shape[1]
    row_out = width // tok_devices
    row_down = ff // tok_devices
    for layer in reversed(range(LAYERS)):
        flat_all, qkv, ctx_here, lse, ctx, summed, gate_up, z, lhs_all = stored[layer]
        z_grad, gain_two, bias_two = jax.vjp(
            layer_norm, z, ln_gain[layer, 1], ln_bias[layer, 1]
        )[1](gradient)
        z_low = z_grad.astype(BF16)
        hidden_grad = dot(z_low, wd[layer], NT)
        gate_grad = jax.vjp(gated_gelu, gate_up)[1](hidden_grad)[0].astype(BF16)
        rhs = jnp.concatenate(
            (
                gate_grad.reshape(tok_count, dp_devices, in_cols),
                z_low.reshape(tok_count, dp_devices, down_cols),
            ),
            axis=-1,
        ).transpose(1, 0, 2)
        rhs_all = lax.all_to_all(rhs, "dp", 0, 0).reshape(dp_devices * tok_count, -1)
        y1_grad = z_grad + dot(gate_grad, wi[layer], NT)
        s_grad, gain_one, bias_one = jax.vjp(
            layer_norm, summed, ln_gain[layer, 0], ln_bias[layer, 0]
        )[1](y1_grad)
        small += [gain_one, gain_two, bias_one, bias_two]
        s_low = s_grad.astype(BF16)
        ctx_grad = dot(s_low, wo[layer], NT).astype(BF16)
        ctx_grad = spread(ctx_grad.reshape(tok_count, sub, cols).transpose(1, 0, 2))
        ctx_grad = ctx_grad.reshape(full_len, cols)
        head_grad = attend_backward(qkv, ctx_here, ctx_grad, lse, far_dist, slopes)
        g_in = dot(lhs_all[:, :width], rhs_all[:, :in_cols], TN).astype(BF16)
        g_down = dot(lhs_all[:, width:], rhs_all[:, in_cols:], TN).astype(BF16)
        g_in = reduce_tok(g_in.reshape(tok_devices, row_out, in_cols))
        g_down = reduce_tok(g_down.reshape(tok_devices, row_down, down_cols))
        g_in = gather_dp(g_in).transpose(1, 0, 2).reshape(row_out, -1)
        g_down = gather_dp(g_down).transpose(1, 0, 2).reshape(row_down, -1)
        g_qkv = dot(flat_all, head_grad, TN).astype(BF16)
        back = spread(head_grad.reshape(sub, tok_count, 3 * cols))
        back = back.reshape(sub, tok_count, 3, cols).transpose(1, 2, 0, 3).reshape(tok_count, -1)
        gradient = s_grad + dot(back, wq[layer], NT)
        g_qkv = g_qkv.reshape(seq_count, sub, row_out, 3 * cols)
        for bit in range(bits_of("dp")):
            g_qkv = g_qkv.reshape(seq_count, sub, -1, 2, g_qkv.shape[2] // 2, 3 * cols)
            g_qkv = reduce_half(g_qkv, "dp", bit, 3)
            g_qkv = g_qkv.reshape(seq_count, sub, -1, 3 * cols)
        for bit in range(bits_of("tok")):
            if (1 << bit) >= sub:
                g_qkv = g_qkv.reshape(-1, 2, *g_qkv.shape[1:])
                g_qkv = reduce_half(g_qkv, "tok", bit, 1)
        g_qkv = g_qkv[0]
        for bit in reversed(range(bits_of("dp"))):
            g_qkv = gather_pair(g_qkv, "dp", bit, 1).reshape(sub, -1, 3 * cols)
        g_qkv = spread(g_qkv).reshape(sub, row_out, 3, cols)
        g_qkv = g_qkv.transpose(1, 2, 0, 3).reshape(row_out, -1)
        g_out = dot(ctx, s_low, TN).astype(BF16).reshape(tok_devices, row_out, width)
        g_out = reduce_tok(g_out)
        for bit in range(bits_of("dp")):
            g_out = (g_out.astype(F32) + swap(g_out, "dp", bit).astype(F32)).astype(BF16)
        outs[layer] = tuple(v.astype(F32) for v in (g_qkv, g_out, g_in, g_down))
    grad_tokens = jnp.where(masked, 0.0, gradient).astype(BF16)
    grad_tokens = regroup(grad_tokens.reshape(seq_count, local_len, width)).astype(F32)
    small.append(jnp.sum(jnp.where(masked, gradient, 0.0), axis=0))
    small = lax.all_gather(jnp.stack(small, axis=0), ("dp", "tok"))
    small = jnp.sum(small, axis=0)
    small = lax.dynamic_slice_in_dim(small, tok_place * row_out, row_out, 1)
    by_layer = jnp.flip(small[: 4 * LAYERS].reshape(LAYERS, 2, 2, row_out), axis=0)
    return (
        layer_out,
        grad_tokens,
        small[-1],
        *(jnp.stack([outs[i][n] for i in range(LAYERS)], axis=1) for n in range(4)),
        by_layer[:, 0],
        by_layer[:, 1],
    )


def solution(mesh):
    in_specs = (
        P("dp", "tok", None),
        P("dp", "tok"),
        P("dp", "tok"),
        P(),
        P(),
        P(),
        P(),
        P(),
        P(),
        P(),
        P("dp", "tok", None),
    )
    out_specs = (
        P("dp", "tok", None),
        P("dp", "tok", None),
        P("tok"),
        P("tok", None, None),
        P("tok", None, None),
        P("tok", None, None),
        P("tok", None, None),
        P(None, None, "tok"),
        P(None, None, "tok"),
    )
    return jax.shard_map(
        per_device, mesh=mesh, in_specs=in_specs, out_specs=out_specs, check_vma=False
    )
```

time: 1850 us -> 839 us (0.45)
  waiting for transfers between devices: 1000 us -> 172 us
  matrix products: 290 us -> 98 us
  local copies, waits for them, and re-layouts: 271 us -> 131 us
  Pallas kernels: 0 us -> 90.1 us
  starting transfers between devices: 35.8 us -> 109 us
  blocking collectives: 92.5 us -> 125 us
  other arithmetic: 115 us -> 87.6 us
    reduce_scatter x3 -> x0, waiting for transfers between devices: 553 us -> none  [the longest x1 317 us: per_device(): lax.psum_scatter(members[2].astype(jnp.bfloat16), 'tok', scatter_dimensio...]
    unnamed x10 -> x2, waiting for transfers between devices: 305 us -> 0.03 us
    dot_general x106 -> x24, matrix products: 287 us -> 98 us  [dot(): return lax.dot_general(a, b, (dims, ((), ())), preferred_element_type=F32)]
    ppermute x0 -> x40, waiting for transfers between devices: none -> 165 us  [swap(): lax.ppermute(value, axis, [(i, i ^ 1 << bit) for i in range(lax.axis_size...]
    slice x15 -> x5, local copies, waits for them, and re-layouts: 109 us -> 2.61 us  [the longest x1 2.46 us: per_device(): qkv = dot(flat_all, wq_mine[layer], NN).astype(BF16)]
    pallas_call x0 -> x8, Pallas kernels: none -> 90.1 us  [the longest x4 41.7 us: split_layers(): pl.pallas_call(body, grid=(rows // row_block, cols // col_block), in_spec...]
    all_to_all x7 -> x13, waiting for transfers between devices: 82.4 us -> 6.87 us  [the longest x8 6.86 us: spread(): return lax.all_to_all(value, 'tok', 0, 0, axis_index_groups=near)]
    psum x1 -> x0, waiting for transfers between devices: 64.4 us -> none  [per_device(): lax.psum(shares[1].astype(jnp.bfloat16), 'dp').astype(jnp.float32)]
  transfers between devices with their start and end apart: 14 -> 55, of which waited for: 12 -> 22; matrix products, arithmetic and copies ran while one was open for 8% -> 28% of each run, Pallas kernels for 0% -> 8%
where the time goes in v1:
time: 839 us; the launch traced here: 828 us
  waiting for transfers between devices  172 us (21%)
  local copies, waits for them, and re-layouts  131 us (16%)
  blocking collectives  125 us (15%)
  starting transfers between devices  109 us (13%)
  matrix products  98 us (12%)
  Pallas kernels  90.1 us (11%)
  other arithmetic  87.6 us (10%)
  between operations  15.9 us (2%)
    ppermute x40, waiting for transfers between devices, swap(): lax.ppermute(value, axis, [(i, i ^ 1 << bit) for i in range(lax.axis_size...  165 us
    dot_general x24, matrix products, dot(): return lax.dot_general(a, b, (dims, ((), ())), preferred_element_type=F32)  98 us
    all_gather x1, blocking collectives, per_device(): small = lax.all_gather(jnp.stack(small, axis=0), ('dp', 'tok'))  76 us
    ppermute x40, starting transfers between devices, swap(): lax.ppermute(value, axis, [(i, i ^ 1 << bit) for i in range(lax.axis_size...  52.9 us
    pallas_call x4, Pallas kernels, split_layers(): pl.pallas_call(body, grid=(rows // row_block, cols // col_block), in_spec...  41.7 us
    all_to_all x8, starting transfers between devices, spread(): return lax.all_to_all(value, 'tok', 0, 0, axis_index_groups=near)  33 us
    all_to_all x2, blocking collectives, spread(): return lax.all_to_all(value, 'tok', 0, 0, axis_index_groups=near)  30.9 us
    pallas_call x2, Pallas kernels, attend_backward(): pl.pallas_call(body, grid=(length // block,), in_specs=[pl.BlockSpec(memo...  25.4 us
  transfers between devices with their start and end apart: 55, of which 22 were waited for; matrix products, arithmetic and copies ran while one was open for 28% of the time, Pallas kernels for 8%

profile of v1, /device:TPU:0, one launch (start us, length us, event | category | flops | bytes accessed | tf_op | source)
XLA Modules:
  0.0 828.4 jit_solution(16910159419456948287)
XLA Ops:
  9.8 18.2 %all_to_all.80 = bf16[2,128,896]{2,1,0:T(8,128)(2,1)S(1)} all-to-all(bf16[2,128,896]{2,1,0:T(8,128)(2,1)S(1)} %pad_maximum_fusion.8), channel_id=1, replica_groups={{0,4},{1,5},{2,6},{3,7},{8,12},{9,13},{10,14},{11,15},{16,20},{17,21},{..., dimensions={0} | all-to-all | bytes 917504 | tf_op jit(solution)/shard_map/all_to_all | solution.py:243
  34.1 8.1 split_layers.4
  42.2 10.3 %copy.244 = bf16[2,768,2304]{1,2,0:T(8,128)(2,1)} copy(bf16[2,768,2304]{2,1,0:T(8,128)(2,1)} %split_layers.4) | data formatting | bytes 14155776 | tf_op jit(solution)/shard_map/split_layers/pallas_call | solution.py:64
  55.7 13.0 %split_layers.7 = bf16[2,3072,768]{2,1,0:T(8,128)(2,1)} custom-call(bf16[3072,2,768]{2,1,0:T(2,128)(2,1)} %in_ref.7), custom_call_target="tpu_custom_call" | custom-call | flops 2415919104 | bytes 18874368 | tf_op jit(solution)/shard_map/split_layers/pallas_call | solution.py:64
  79.1 11.5 %attend_forward.2 = (bf16[1024,192]{1,0:T(8,128)(2,1)}, f32[3,1024]{1,0:T(4,128)}) custom-call(f32[3]{0:T(128)} %dynamic_slice.142.slope_ref, bf16[1024,576]{1,0:T(8,128)(2,1)} %convolution_convert_fusion.3.qkv_ref, f32[1024,1024]{1,0:T(8,128)} %convert_select_fusion.dist_ref), custom_call_target="tpu_custom_call" | custom-call | flops 3221225472 | bytes 4194304 | tf_op jit(solution)/shard_map/attend_forward/pallas_call | solution.py:99
  101.6 16.1 %split_layers.6 = bf16[2,768,6144]{2,1,0:T(8,128)(2,1)} custom-call(bf16[768,2,6144]{2,1,0:T(2,128)(2,1)} %in_ref.6), custom_call_target="tpu_custom_call" | custom-call | flops 4831838208 | bytes 37748736 | tf_op jit(solution)/shard_map/split_layers/pallas_call | solution.py:64
  125.6 7.7 multiply_convert_fusion.1
  135.4 22.0 %all_to_all.81 = bf16[4,256,768]{2,1,0:T(8,128)(2,1)S(1)} all-to-all(bf16[4,256,768]{2,1,0:T(8,128)(2,1)S(1)} %broadcast_in_dim.61), channel_id=1, replica_groups={{0,1,2,3},{4,5,6,7},{8,9,10,11},{12,13,14,15},{16,17,18,19},{20,21,22,2..., dimensions={0} | all-to-all | bytes 3145728 | tf_op jit(solution)/shard_map/all_to_all | solution.py:246
  161.2 11.6 %attend_forward.3 = (bf16[1024,192]{1,0:T(8,128)(2,1)}, f32[3,1024]{1,0:T(4,128)}) custom-call(f32[3]{0:T(128)} %dynamic_slice.142.slope_ref, bf16[1024,576]{1,0:T(8,128)(2,1)} %convolution_convert_fusion.2.qkv_ref, f32[1024,1024]{1,0:T(8,128)} %convert_select_fusion.dist_ref), custom_call_target="tpu_custom_call" | custom-call | flops 3221225472 | bytes 4194304 | tf_op jit(solution)/shard_map/attend_forward/pallas_call | solution.py:99
  174.0 8.8 %all_to_all.82 = bf16[4,256,192]{1,2,0:T(8,128)(2,1)S(1)} all-to-all(bf16[4,256,192]{1,2,0:T(8,128)(2,1)S(1)} %copy.248), channel_id=1, replica_groups={{0,1,2,3},{4,5,6,7},{8,9,10,11},{12,13,14,15},{16,17,18,19},{20,21,22,2..., dimensions={0} | all-to-all | bytes 786432 | tf_op jit(solution)/shard_map/all_to_all | solution.py:246
  194.8 7.7 multiply_convert_fusion
  206.3 9.3 %fusion.54 = (f32[256,3072]{1,0:T(8,128)}, f32[256,3072]{1,0:T(8,128)}) fusion(f32[256,3072]{1,0:T(8,128)S(1)} %copy-done.9, f32[256,6144]{1,0:T(8,128)} %copy-done.2, bf16[256,768]{1,0:T(8,128)(2,1)S(1)} %add_convert_fusion.6, bf16[2,3072,768]{2,1,0:T(8,128)(2,1)} %split_layers.7), kind=kOutput, calls=%fused_computation.119 | convolution fusion | flops 1220542464 | bytes 20840448 | tf_op jit(solution)/shard_map/dot_general | solution.py:39
  243.4 12.7 %attend_backward.2 = bf16[1024,576]{1,0:T(8,128)(2,1)} custom-call(f32[3]{0:T(128)} %dynamic_slice.142.slope_ref, bf16[1024,576]{1,0:T(8,128)(2,1)} %convolution_convert_fusion.2.qkv_ref, bf16[1024,192]{1,0:T(8,128)(2,1)} %get-tuple-element.38.ctx_ref, bf16[1024,192]{1,0:T(8,128)(2,1)} %bitcast.477, f32[3,1024]{1,0:T(4,128)} %get-tuple-element.39.lse_ref, ...), custom_call_target="tpu_custom_call" | custom-call | flops 8053063680 | bytes 4194304 | tf_op jit(solution)/shard_map/attend_backward/pallas_call | solution.py:163
  291.5 7.6 collective-permute-done.8
  316.1 9.0 %fusion.55 = (f32[256,3072]{1,0:T(8,128)}, f32[256,3072]{1,0:T(8,128)}) fusion(f32[256,3072]{1,0:T(8,128)S(1)} %copy-done.8, f32[256,6144]{1,0:T(8,128)} %copy-done.1, bf16[256,768]{1,0:T(8,128)(2,1)S(1)} %add_convert_fusion.4, bf16[2,3072,768]{2,1,0:T(8,128)(2,1)} %split_layers.7), kind=kOutput, calls=%fused_computation.120 | convolution fusion | flops 1220542464 | bytes 20840448 | tf_op jit(solution)/shard_map/dot_general | solution.py:39
  373.0 12.7 %attend_backward.3 = bf16[1024,576]{1,0:T(8,128)(2,1)} custom-call(f32[3]{0:T(128)} %dynamic_slice.142.slope_ref, bf16[1024,576]{1,0:T(8,128)(2,1)} %convolution_convert_fusion.3.qkv_ref, bf16[1024,192]{1,0:T(8,128)(2,1)} %get-tuple-element.37.ctx_ref, bf16[1024,192]{1,0:T(8,128)(2,1)} %bitcast.476, f32[3,1024]{1,0:T(4,128)} %get-tuple-element.40.lse_ref, ...), custom_call_target="tpu_custom_call" | custom-call | flops 8053063680 | bytes 4194304 | tf_op jit(solution)/shard_map/attend_backward/pallas_call | solution.py:163
  457.3 7.6 collective-permute-done.11
  486.5 29.0 %collective-permute-done.19 = bf16[96,768]{1,0:T(8,128)(2,1)S(1)} collective-permute-done((bf16[96,768]{1,0:T(8,128)(2,1)S(1)}, bf16[96,768]{1,0:T(8,128)(2,1)S(1)}, u32[]{:S(2)}, u32[]{:S(2)}) %collective-permute-start.19) | collective-permute-done | bytes 147488 | tf_op jit(solution)/shard_map/ppermute | solution.py:188
  543.6 76.0 %all-gather.1 = f32[32,9,768]{2,1,0:T(8,128)S(1)} all-gather(f32[1,9,768]{2,1,0:T(8,128)S(1)} %bitcast.478), channel_id=2, replica_groups=mesh['dp'=4,'tok'=8] {'dp','tok'}, dimensions={0}, use_global_device_ids=true | all-gather | bytes 912384 | tf_op jit(solution)/shard_map/all_gather | solution.py:362
  651.8 7.9 collective-permute-done.30
  671.1 7.4 collective-permute-done.20
  728.8 26.3 %collective-permute-done.35 = bf16[4,384,192]{1,2,0:T(8,128)(2,1)S(1)} collective-permute-done((bf16[4,384,192]{1,2,0:T(8,128)(2,1)S(1)}, bf16[4,384,192]{1,2,0:T(8,128)(2,1)S(1)}, u32[]{:S(2)}, u32[]{:S(2)}) %collective-permute-start.35) | collective-permute-done | bytes 589856 | tf_op jit(solution)/shard_map/ppermute | solution.py:188
  768.4 11.0 %collective-permute-done.26 = bf16[2,96,1536]{2,1,0:T(8,128)(2,1)S(1)} collective-permute-done((bf16[2,96,1536]{2,1,0:T(8,128)(2,1)S(1)}, bf16[2,96,1536]{2,1,0:T(8,128)(2,1)S(1)}, u32[]{:S(2)}, u32[]{:S(2)}) %collective-permute-start.26) | collective-permute-done | bytes 589856 | tf_op jit(solution)/shard_map/ppermute | solution.py:188
  784.0 10.9 %collective-permute-done.27 = bf16[1,96,1536]{2,1,0:T(8,128)(2,1)S(1)} collective-permute-done((bf16[1,96,1536]{2,1,0:T(8,128)(2,1)S(1)}, bf16[1,96,1536]{2,1,0:T(8,128)(2,1)S(1)}, u32[]{:S(2)}, u32[]{:S(2)}) %collective-permute-start.27) | collective-permute-done | bytes 294944 | tf_op jit(solution)/shard_map/ppermute | solution.py:188
  (475 shorter events, 449.9 us)
Async XLA Ops:
  30.5 38.1 %all-to-all-start.1 = ((bf16[4,256,896]{1,2,0:T(8,128)(2,1)}), bf16[4,256,896]{1,2,0:T(8,128)(2,1)S(1)}, u32[]{:S(2)}, u32[]{:S(2)}) async-start(bf16[4,256,896]{1,2,0:T(8,128)(2,1)} %broadcast_in_dim.59), calls=%async_computation.1 | async-start | bytes 3670016 | tf_op jit(solution)/shard_map/all_to_all | solution.py:246
  92.7 25.0 %all-to-all-start.2 = ((bf16[4,256,192]{1,2,0:T(8,128)(2,1)}), bf16[4,256,192]{1,2,0:T(8,128)(2,1)S(1)}, u32[]{:S(2)}, u32[]{:S(2)}) async-start(bf16[4,256,192]{1,2,0:T(8,128)(2,1)} %copy.246), calls=%async_computation.2 | async-start | bytes 786432 | tf_op jit(solution)/shard_map/all_to_all | solution.py:246
  182.8 21.5 %all-to-all-start.6 = ((bf16[2,128,768]{2,1,0:T(8,128)(2,1)}), bf16[2,128,768]{2,1,0:T(8,128)(2,1)S(1)}, u32[]{:S(2)}, u32[]{:S(2)}) async-start(bf16[2,128,768]{2,1,0:T(8,128)(2,1)} %param.25), calls=%async_computation.6 | async-start | bytes 786432 | tf_op jit(solution)/shard_map/all_to_all | solution.py:243
  236.6 393.6 %all-gather.5.cloned.1.call-start = ((), (), s32[]{:S(2)}) async-start(), calls=%async_computation.16 | async-start | bytes 9830400 | tf_op jit(solution)/shard_map/all_gather | solution.py:292
  270.6 34.1 %all-to-all-start.8 = ((bf16[4,256,576]{1,2,0:T(8,128)(2,1)}), bf16[4,256,576]{1,2,0:T(8,128)(2,1)S(1)}, u32[]{:S(2)}, u32[]{:S(2)}) async-start(bf16[4,256,576]{1,2,0:T(8,128)(2,1)} %copy.251), calls=%async_computation.8 | async-start | bytes 2359296 | tf_op jit(solution)/shard_map/all_to_all | solution.py:246
  302.1 59.1 %collective-permute-start.15 = (bf16[4,96,768]{2,1,0:T(8,128)(2,1)}, bf16[4,96,768]{2,1,0:T(8,128)(2,1)}, u32[]{:S(2)}, u32[]{:S(2)}) collective-permute-start(bf16[4,96,768]{2,1,0:T(8,128)(2,1)} %dynamic-slice_bitcast_fusion.4), channel_id=1, source_target_pairs={{0,1},{1,0},{2,3},{3,2},{4,5},{5,4},{6,7},{7,6},{8,9},{9,8},{10,11... | collective-permute-start | bytes 1769480 | tf_op jit(solution)/shard_map/ppermute | solution.py:188
  304.7 32.5 %all-to-all-start.5 = ((bf16[2,128,768]{2,1,0:T(8,128)(2,1)}), bf16[2,128,768]{2,1,0:T(8,128)(2,1)}, u32[]{:S(2)}, u32[]{:S(2)}) async-start(bf16[2,128,768]{2,1,0:T(8,128)(2,1)} %bitcast.458), calls=%async_computation.5 | async-start | bytes 786432 | tf_op jit(solution)/shard_map/all_to_all | solution.py:243
  363.3 45.3 %all-to-all-start.15 = ((bf16[4,256,1728]{1,2,0:T(8,128)(2,1)}), bf16[4,256,1728]{1,2,0:T(8,128)(2,1)S(1)}, u32[]{:S(2)}, u32[]{:S(2)}) async-start(bf16[4,256,1728]{1,2,0:T(8,128)(2,1)} %maximum_bitcast_fusion.1), calls=%async_computation.15 | async-start | bytes 7077888 | tf_op jit(solution)/shard_map/all_to_all | solution.py:319
  367.0 340.4 %all-gather.7.cloned.1.call-start = ((), (), s32[]{:S(2)}) async-start(), calls=%async_computation.17 | async-start | bytes 9830400 | tf_op jit(solution)/shard_map/all_gather | solution.py:292
  369.0 27.9 %collective-permute-start.16 = (bf16[2,96,768]{2,1,0:T(8,128)(2,1)}, bf16[2,96,768]{2,1,0:T(8,128)(2,1)}, u32[]{:S(2)}, u32[]{:S(2)}) collective-permute-start(bf16[2,96,768]{2,1,0:T(8,128)(2,1)} %dynamic-slice_bitcast_fusion.10), channel_id=1, source_target_pairs={{0,2},{1,3},{2,0},{3,1},{4,6},{5,7},{6,4},{7,5},{8,10},{9,11},{10,... | collective-permute-start | bytes 884744 | tf_op jit(solution)/shard_map/ppermute | solution.py:188
  408.6 37.3 %all-to-all-start.10 = ((bf16[4,256,576]{1,2,0:T(8,128)(2,1)}), bf16[4,256,576]{1,2,0:T(8,128)(2,1)}, u32[]{:S(2)}, u32[]{:S(2)}) async-start(bf16[4,256,576]{1,2,0:T(8,128)(2,1)} %copy.255), calls=%async_computation.10 | async-start | bytes 2359296 | tf_op jit(solution)/shard_map/all_to_all | solution.py:246
  424.1 18.5 %collective-permute-start.10 = (bf16[4,96,768]{2,1,0:T(8,128)(2,1)}, bf16[4,96,768]{2,1,0:T(8,128)(2,1)}, u32[]{:S(2)}, u32[]{:S(2)}) collective-permute-start(bf16[4,96,768]{2,1,0:T(8,128)(2,1)} %dynamic-slice_bitcast_fusion.5), channel_id=1, source_target_pairs={{0,1},{1,0},{2,3},{3,2},{4,5},{5,4},{6,7},{7,6},{8,9},{9,8},{10,11... | collective-permute-start | bytes 1769480 | tf_op jit(solution)/shard_map/ppermute | solution.py:188
  431.5 42.8 %collective-permute-start.17 = (bf16[1,96,768]{2,1,0:T(8,128)(2,1)}, bf16[1,96,768]{2,1,0:T(8,128)(2,1)}, u32[]{:S(2)}, u32[]{:S(2)}) collective-permute-start(bf16[1,96,768]{2,1,0:T(8,128)(2,1)} %constant_dynamic-slice_fusion.9), channel_id=1, source_target_pairs={{0,4},{1,5},{2,6},{3,7},{4,0},{5,1},{6,2},{7,3},{8,12},{9,13},{10,... | collective-permute-start | bytes 442376 | tf_op jit(solution)/shard_map/ppermute | solution.py:188
  445.9 19.7 %all-to-all-start.12 = ((bf16[4,96,576]{2,1,0:T(8,128)(2,1)}), bf16[4,96,576]{2,1,0:T(8,128)(2,1)}, u32[]{:S(2)}, u32[]{:S(2)}) async-start(bf16[4,96,576]{2,1,0:T(8,128)(2,1)} %bitcast.451), calls=%async_computation.12 | async-start | bytes 983040 | tf_op jit(solution)/shard_map/all_to_all | solution.py:246
  465.7 153.9 %all-to-all-start.14 = ((bf16[4,256,1728]{1,2,0:T(8,128)(2,1)}), bf16[4,256,1728]{1,2,0:T(8,128)(2,1)}, u32[]{:S(2)}, u32[]{:S(2)}) async-start(bf16[4,256,1728]{1,2,0:T(8,128)(2,1)} %maximum_bitcast_fusion), calls=%async_computation.14 | async-start | bytes 7077888 | tf_op jit(solution)/shard_map/all_to_all | solution.py:319
  482.9 32.6 %collective-permute-start.19 = (bf16[96,768]{1,0:T(8,128)(2,1)S(1)}, bf16[96,768]{1,0:T(8,128)(2,1)S(1)}, u32[]{:S(2)}, u32[]{:S(2)}) collective-permute-start(bf16[96,768]{1,0:T(8,128)(2,1)S(1)} %add_convert_fusion.12), channel_id=1, source_target_pairs={{0,16},{8,24},{16,0},{24,8},{1,17},{9,25},{17,1},{25,9},{2,18},{10... | collective-permute-start | bytes 442376 | tf_op jit(solution)/shard_map/ppermute | solution.py:188
  485.3 46.1 %collective-permute-start.14 = (bf16[96,768]{1,0:T(8,128)(2,1)}, bf16[96,768]{1,0:T(8,128)(2,1)}, u32[]{:S(2)}, u32[]{:S(2)}) collective-permute-start(bf16[96,768]{1,0:T(8,128)(2,1)} %add_convert_fusion.15), channel_id=1, source_target_pairs={{0,16},{8,24},{16,0},{24,8},{1,17},{9,25},{17,1},{25,9},{2,18},{10... | collective-permute-start | bytes 442376 | tf_op jit(solution)/shard_map/ppermute | solution.py:188
  619.6 80.8 %all-to-all-start.11 = ((bf16[2,128,768]{2,1,0:T(8,128)(2,1)}), bf16[2,128,768]{2,1,0:T(8,128)(2,1)}, u32[]{:S(2)}, u32[]{:S(2)}) async-start(bf16[2,128,768]{2,1,0:T(8,128)(2,1)} %bitcast.39), calls=%async_computation.11 | async-start | bytes 786432 | tf_op jit(solution)/shard_map/all_to_all | solution.py:243
  649.6 29.0 %collective-permute-start.20 = (bf16[4,96,1536]{2,1,0:T(8,128)(2,1)}, bf16[4,96,1536]{2,1,0:T(8,128)(2,1)}, u32[]{:S(2)}, u32[]{:S(2)}) collective-permute-start(bf16[4,96,1536]{2,1,0:T(8,128)(2,1)} %dynamic-slice_bitcast_fusion.1), channel_id=1, source_target_pairs={{0,1},{1,0},{2,3},{3,2},{4,5},{5,4},{6,7},{7,6},{8,9},{9,8},{10,11... | collective-permute-start | bytes 3538952 | tf_op jit(solution)/shard_map/ppermute | solution.py:188
  707.5 20.2 %collective-permute-start.23 = (bf16[1,96,1536]{2,1,0:T(8,128)(2,1)}, bf16[1,96,1536]{2,1,0:T(8,128)(2,1)}, u32[]{:S(2)}, u32[]{:S(2)}) collective-permute-start(bf16[1,96,1536]{2,1,0:T(8,128)(2,1)} %add_convert_fusion.8), channel_id=1, source_target_pairs={{0,16},{8,24},{16,0},{24,8},{1,17},{9,25},{17,1},{25,9},{2,18},{10... | collective-permute-start | bytes 884744 | tf_op jit(solution)/shard_map/ppermute | solution.py:188
  713.7 43.3 %collective-permute-start.25 = (bf16[4,96,1536]{2,1,0:T(8,128)(2,1)}, bf16[4,96,1536]{2,1,0:T(8,128)(2,1)}, u32[]{:S(2)}, u32[]{:S(2)}) collective-permute-start(bf16[4,96,1536]{2,1,0:T(8,128)(2,1)} %dynamic-slice_bitcast_fusion), channel_id=1, source_target_pairs={{0,1},{1,0},{2,3},{3,2},{4,5},{5,4},{6,7},{7,6},{8,9},{9,8},{10,11... | collective-permute-start | bytes 3538952 | tf_op jit(solution)/shard_map/ppermute | solution.py:188
  726.6 28.4 %collective-permute-start.35 = (bf16[4,384,192]{1,2,0:T(8,128)(2,1)S(1)}, bf16[4,384,192]{1,2,0:T(8,128)(2,1)S(1)}, u32[]{:S(2)}, u32[]{:S(2)}) collective-permute-start(bf16[4,384,192]{1,2,0:T(8,128)(2,1)S(1)} %bitcast.473), channel_id=1, source_target_pairs={{0,1},{1,0},{2,3},{3,2},{4,5},{5,4},{6,7},{7,6},{8,9},{9,8},{10,11... | collective-permute-start | bytes 1769480 | tf_op jit(solution)/shard_map/ppermute | solution.py:188
  758.6 20.8 %collective-permute-start.26 = (bf16[2,96,1536]{2,1,0:T(8,128)(2,1)S(1)}, bf16[2,96,1536]{2,1,0:T(8,128)(2,1)S(1)}, u32[]{:S(2)}, u32[]{:S(2)}) collective-permute-start(bf16[2,96,1536]{2,1,0:T(8,128)(2,1)S(1)} %dynamic-slice_bitcast_fusion.2), channel_id=1, source_target_pairs={{0,2},{1,3},{2,0},{3,1},{4,6},{5,7},{6,4},{7,5},{8,10},{9,11},{10,... | collective-permute-start | bytes 1769480 | tf_op jit(solution)/shard_map/ppermute | solution.py:188
  759.1 23.3 %collective-permute-start.24 = (bf16[2,96,1536]{2,1,0:T(8,128)(2,1)S(1)}, bf16[2,96,1536]{2,1,0:T(8,128)(2,1)S(1)}, u32[]{:S(2)}, u32[]{:S(2)}) collective-permute-start(bf16[2,96,1536]{2,1,0:T(8,128)(2,1)S(1)} %maximum_bitcast_fusion.2), channel_id=1, source_target_pairs={{0,8},{8,0},{16,24},{24,16},{1,9},{9,1},{17,25},{25,17},{2,10},{10... | collective-permute-start | bytes 1769480 | tf_op jit(solution)/shard_map/ppermute | solution.py:188
  (103 other events, 1007.7 us)
Sparse Core Ops, SparseCore 0:
  240.0 65.0 all-gather.4
  397.0 62.9 all-gather.6

commit v2 on v1

v2 whole, which is shorter than its diff:
```python
import math

import jax
import jax.numpy as jnp
from jax import lax
from jax.experimental import pallas as pl
from jax.experimental.pallas import tpu as pltpu
from jax.sharding import PartitionSpec as P

HEADS = 12
HEAD_DIM = 64
LAYERS = 2
LANES = 128
PACK = 384
SCALE = 1.0 / math.sqrt(HEAD_DIM)
FAR = 1e30
BF16 = jnp.bfloat16
F32 = jnp.float32
VMEM_LIMIT = 56 << 20
COST_TIMES = 4


def alibi_slopes(head_count):
    head_index = jnp.arange(head_count, dtype=jnp.float32)
    return jnp.exp2(jnp.where(head_index < 8.0, -(head_index + 1.0), 7.5 - head_index))


def dot(a, b, dims):
    return lax.dot_general(a, b, (dims, ((), ())), preferred_element_type=F32)


def cost(flops, bytes_accessed, transcendentals):
    return pl.CostEstimate(
        flops=COST_TIMES * flops,
        bytes_accessed=bytes_accessed,
        transcendentals=transcendentals,
    )


NN = ((1,), (0,))
NT = ((1,), (1,))
TN = ((0,), (0,))


def split_layers(weight):
    rows, _, cols = weight.shape
    row_block = 256
    col_block = next(c for c in (3072, 2304, 1152, 768) if cols % c == 0)

    def body(in_ref, out_ref):
        to_row = lax.broadcasted_iota(jnp.int32, (256, 256), 0)
        from_row = lax.broadcasted_iota(jnp.int32, (256, 256), 1)
        wanted = jnp.where(to_row < 128, 2 * to_row, 2 * to_row - 255)
        pick = jnp.where(from_row == wanted, 1.0, 0.0).astype(BF16)
        for part in range(row_block // 128):
            at = slice(part * 128, part * 128 + 128)
            mixed = in_ref[at].reshape(256, col_block)
            picked = dot(pick, mixed, NN).astype(BF16)
            out_ref[0, at] = picked[:128]
            out_ref[1, at] = picked[128:]

    return pl.pallas_call(
        body,
        grid=(rows // row_block, cols // col_block),
        in_specs=[pl.BlockSpec((row_block, 2, col_block), lambda i, j: (i, 0, j))],
        out_specs=pl.BlockSpec((2, row_block, col_block), lambda i, j: (0, i, j)),
        out_shape=jax.ShapeDtypeStruct((2, rows, cols), BF16),
        compiler_params=pltpu.CompilerParams(vmem_limit_bytes=VMEM_LIMIT),
        cost_estimate=cost(
            flops=2 * 512 * rows * cols, bytes_accessed=8 * rows * cols, transcendentals=0
        ),
        name="split_layers",
    )(weight)


def split_layers_by_group(weight, sub):
    rows, _, cols = weight.shape
    row_block = 256
    group_cols = cols // sub // 3

    def body(in_ref, out_ref):
        to_row = lax.broadcasted_iota(jnp.int32, (256, 256), 0)
        from_row = lax.broadcasted_iota(jnp.int32, (256, 256), 1)
        wanted = jnp.where(to_row < 128, 2 * to_row, 2 * to_row - 255)
        pick = jnp.where(from_row == wanted, 1.0, 0.0).astype(BF16)
        for part in range(row_block // 128):
            at = slice(part * 128, part * 128 + 128)
            picked = dot(pick, in_ref[at].reshape(256, cols), NN).astype(BF16)
            for j in range(sub):
                for n in range(3):
                    first = (n * sub + j) * group_cols
                    block = picked[:, first : first + group_cols]
                    to = slice(n * group_cols, n * group_cols + group_cols)
                    out_ref[0, j, at, to] = block[:128]
                    out_ref[1, j, at, to] = block[128:]

    return pl.pallas_call(
        body,
        grid=(rows // row_block,),
        in_specs=[pl.BlockSpec((row_block, 2, cols), lambda i: (i, 0, 0))],
        out_specs=pl.BlockSpec((2, sub, row_block, 3 * group_cols), lambda i: (0, 0, i, 0)),
        out_shape=jax.ShapeDtypeStruct((2, sub, rows, 3 * group_cols), BF16),
        compiler_params=pltpu.CompilerParams(vmem_limit_bytes=VMEM_LIMIT),
        cost_estimate=cost(
            flops=2 * 512 * rows * cols, bytes_accessed=8 * rows * cols, transcendentals=0
        ),
        name="split_qkv",
    )(weight)


def norm_parts(value):
    center = jnp.mean(value, axis=-1, keepdims=True)
    shifted = value - center
    inverse = lax.rsqrt(jnp.mean(shifted * shifted, axis=-1, keepdims=True) + 1e-12)
    return shifted * inverse, inverse


def norm_grad(grad, value, gain):
    normed, inverse = norm_parts(value)
    scaled = grad * gain
    one = jnp.mean(scaled, axis=-1, keepdims=True)
    two = jnp.mean(scaled * normed, axis=-1, keepdims=True)
    in_grad = inverse * (scaled - one - normed * two)
    gain_grad = jnp.sum(grad * normed, axis=0, keepdims=True)
    bias_grad = jnp.sum(grad, axis=0, keepdims=True)
    return in_grad, gain_grad, bias_grad


def feed_forward(layer, group, current, ctx, w_out, w_in, w_down, gain, bias):
    count, width = current.shape
    sub, cols = len(ctx), ctx[0].shape[0]
    ff = w_down.shape[1]
    chunk = 768
    steps = ff // chunk

    def body(group_ref, *refs):
        ctx_refs = refs[:sub]
        cur_ref, wo_ref, wg_ref, wu_ref, wd_ref, gain_ref, bias_ref = refs[sub : sub + 7]
        lhs_ref, a_ref, b_ref, sum_ref, z_ref, next_ref, low_ref = refs[sub + 7 : sub + 14]
        y1l_ref, acc_ref, held_ref = refs[sub + 14 :]
        step = pl.program_id(0)

        @pl.when(step == 0)
        def _():
            branch = jnp.zeros((count, width), F32)
            for r in range(sub):
                held_ref[jnp.bitwise_xor(group_ref[0], r)] = ctx_refs[r][...]
            for j in range(sub):
                part = held_ref[j]
                to = slice(j * cols, j * cols + cols)
                lhs_ref[:, width + ff + j * cols : width + ff + j * cols + cols] = (
                    part.astype(F32).T.astype(BF16)
                )
                branch += dot(part, wo_ref[0, to, :], TN)
            summed = cur_ref[...] + branch
            sum_ref[...] = summed
            normed, _ = norm_parts(summed)
            y1 = normed * gain_ref[layer, 0:1, :] + bias_ref[layer, 0:1, :]
            acc_ref[...] = y1
            y1l_ref[...] = y1.astype(BF16)
            lhs_ref[:, :width] = y1.astype(BF16)

        y1l = y1l_ref[...]
        gate = dot(y1l, wg_ref[0], NN)
        up = dot(y1l, wu_ref[0], NN)
        cdf = 0.5 * (1.0 + lax.erf(gate * (0.5**0.5)))
        density = jnp.exp(-0.5 * gate * gate) * (1.0 / math.sqrt(2.0 * math.pi))
        gelu = gate * cdf
        hidden = (gelu * up).astype(BF16)
        a_ref[...] = gelu.astype(BF16)
        b_ref[...] = (up * (cdf + gate * density)).astype(BF16)
        lhs_ref[:, pl.ds(pl.multiple_of(width + step * chunk, 128), chunk)] = hidden
        acc_ref[...] += dot(hidden, wd_ref[0], NN)

        @pl.when(step == steps - 1)
        def _():
            z = acc_ref[...]
            z_ref[...] = z
            normed, _ = norm_parts(z)
            out = normed * gain_ref[layer, 1:2, :] + bias_ref[layer, 1:2, :]
            next_ref[...] = out
            low_ref[...] = out.astype(BF16)

    whole = lambda *shape: pl.BlockSpec(shape, lambda i: (0,) * len(shape))
    return pl.pallas_call(
        body,
        grid=(steps,),
        in_specs=[
            pl.BlockSpec(memory_space=pltpu.SMEM),
            *[whole(cols, count)] * sub,
            whole(count, width),
            pl.BlockSpec((1, width, width), lambda i: (layer, 0, 0)),
            pl.BlockSpec((1, width, chunk), lambda i: (layer, 0, i)),
            pl.BlockSpec((1, width, chunk), lambda i: (layer, 0, steps + i)),
            pl.BlockSpec((1, chunk, width), lambda i: (layer, i, 0)),
            whole(*gain.shape),
            whole(*bias.shape),
        ],
        out_specs=[
            whole(count, ff + 2 * width),
            pl.BlockSpec((count, chunk), lambda i: (0, i)),
            pl.BlockSpec((count, chunk), lambda i: (0, i)),
            whole(count, width),
            whole(count, width),
            whole(count, width),
            whole(count, width),
        ],
        out_shape=[
            jax.ShapeDtypeStruct((count, ff + 2 * width), BF16),
            jax.ShapeDtypeStruct((count, ff), BF16),
            jax.ShapeDtypeStruct((count, ff), BF16),
            jax.ShapeDtypeStruct((count, width), F32),
            jax.ShapeDtypeStruct((count, width), F32),
            jax.ShapeDtypeStruct((count, width), F32),
            jax.ShapeDtypeStruct((count, width), BF16),
        ],
        scratch_shapes=[
            pltpu.VMEM((count, width), BF16),
            pltpu.VMEM((count, width), F32),
            pltpu.VMEM((sub, cols, count), BF16),
        ],
        compiler_params=pltpu.CompilerParams(vmem_limit_bytes=VMEM_LIMIT),
        cost_estimate=cost(
            flops=2 * count * width * (width + 3 * ff),
            bytes_accessed=6 * width * ff + 2 * width * width + count * (20 * width + 6 * ff),
            transcendentals=2 * count * ff,
        ),
        name="feed_forward",
    )(group, *ctx, current, w_out, w_in, w_in, w_down, gain, bias)


def feed_backward(layer, core, group, grad, z, summed, a, b, w_out, w_in, w_down, gain, sub):
    count, width = grad.shape
    ff = w_down.shape[1]
    cols = width // sub
    half = width // 2
    chunk = 768
    steps = ff // chunk

    def body(
        core_ref, group_ref, grad_ref, z_ref, sum_ref, a_ref, b_ref,
        wo_ref, wg_ref, wu_ref, wd_ref, gain_ref, mine_ref, send_ref, ga_ref, small_ref, *refs,
    ):
        gctx_refs = refs[:sub]
        gzl_ref, acc_ref, held_ref = refs[sub:]
        step = pl.program_id(0)
        first = core_ref[0] == 0

        def store(to, low, high):
            mine_ref[:, to] = jnp.where(first, low, high)
            send_ref[:, to] = jnp.where(first, high, low)

        @pl.when(step == 0)
        def _():
            gz, gain_grad, bias_grad = norm_grad(grad_ref[...], z_ref[...], gain_ref[layer, 1:2, :])
            small_ref[1:2, :] = gain_grad
            small_ref[3:4, :] = bias_grad
            acc_ref[...] = gz
            gzl = gz.astype(BF16)
            gzl_ref[...] = gzl
            store(slice(ff, ff + half), gz[:, :half].astype(BF16), gz[:, half:].astype(BF16))

        gzl = gzl_ref[...]
        ghid = dot(gzl, wd_ref[0], NT)
        ggate = (ghid * b_ref[...].astype(F32)).astype(BF16)
        gup = (ghid * a_ref[...].astype(F32)).astype(BF16)
        store(pl.ds(pl.multiple_of(step * chunk, 128), chunk), ggate, gup)
        acc_ref[...] += dot(ggate, wg_ref[0], NT) + dot(gup, wu_ref[0], NT)

        @pl.when(step == steps - 1)
        def _():
            ga, gain_grad, bias_grad = norm_grad(
                acc_ref[...], sum_ref[...], gain_ref[layer, 0:1, :]
            )
            small_ref[0:1, :] = gain_grad
            small_ref[2:3, :] = bias_grad
            ga_ref[...] = ga
            gal = ga.astype(BF16)
            store(slice(ff + half, ff + width), gal[:, :half], gal[:, half:])
            for j in range(sub):
                to = slice(j * cols, j * cols + cols)
                held_ref[j] = dot(wo_ref[0, to, :], gal, NT).astype(BF16)
            for r in range(sub):
                gctx_refs[r][...] = held_ref[jnp.bitwise_xor(group_ref[0], r)]

    whole = lambda *shape: pl.BlockSpec(shape, lambda i: (0,) * len(shape))
    return pl.pallas_call(
        body,
        grid=(steps,),
        in_specs=[
            pl.BlockSpec(memory_space=pltpu.SMEM),
            pl.BlockSpec(memory_space=pltpu.SMEM),
            whole(count, width),
            whole(count, width),
            whole(count, width),
            pl.BlockSpec((count, chunk), lambda i: (0, i)),
            pl.BlockSpec((count, chunk), lambda i: (0, i)),
            pl.BlockSpec((1, width, width), lambda i: (layer, 0, 0)),
            pl.BlockSpec((1, width, chunk), lambda i: (layer, 0, i)),
            pl.BlockSpec((1, width, chunk), lambda i: (layer, 0, steps + i)),
            pl.BlockSpec((1, chunk, width), lambda i: (layer, i, 0)),
            whole(*gain.shape),
        ],
        out_specs=[
            whole(count, ff + width),
            whole(count, ff + width),
            whole(count, width),
            whole(4, width),
            *[whole(cols, count)] * sub,
        ],
        out_shape=[
            jax.ShapeDtypeStruct((count, ff + width), BF16),
            jax.ShapeDtypeStruct((count, ff + width), BF16),
            jax.ShapeDtypeStruct((count, width), F32),
            jax.ShapeDtypeStruct((4, width), F32),
            *[jax.ShapeDtypeStruct((cols, count), BF16)] * sub,
        ],
        scratch_shapes=[
            pltpu.VMEM((count, width), BF16),
            pltpu.VMEM((count, width), F32),
            pltpu.VMEM((sub, cols, count), BF16),
        ],
        compiler_params=pltpu.CompilerParams(vmem_limit_bytes=VMEM_LIMIT),
        cost_estimate=cost(
            flops=2 * count * width * (width + 3 * ff),
            bytes_accessed=6 * width * ff + 2 * width * width + count * (24 * width + 8 * ff),
            transcendentals=0,
        ),
        name="feed_backward",
    )(core, group, grad, z, summed, a, b, w_out, w_in, w_in, w_down, gain)


def pair_grad_in(group, lhs, lhs_other, rhs, rhs_other, ff, tok_devices, sub, far):
    count = lhs.shape[0]
    width = rhs.shape[1] - ff
    rows = width // tok_devices
    seqs = tok_devices // sub
    chunk = 2 * PACK
    steps = ff // chunk
    first_steps = steps - far * PACK // chunk

    def body(group_ref, l1_ref, l2_ref, r1_ref, r2_ref, *refs):
        out_refs, last_ref, held_ref = refs[:sub], refs[sub], refs[sub + 1]
        step = pl.program_id(0)
        out = dot(l1_ref[...], r1_ref[...], TN) + dot(l2_ref[...], r2_ref[...], TN)

        @pl.when(step < first_steps)
        def _():
            for t in range(tok_devices):
                held_ref[t % sub, t // sub] = out[t * rows : t * rows + rows].astype(BF16)
            for r in range(sub):
                out_refs[r][...] = held_ref[jnp.bitwise_xor(group_ref[0], r)]

        @pl.when(step >= first_steps)
        def _():
            for t in range(tok_devices):
                part = out[t * rows : t * rows + rows].astype(BF16)
                for f in range(2):
                    last_ref[t, f] = part[:, f * PACK : f * PACK + PACK]

    return pl.pallas_call(
        body,
        grid=(steps,),
        in_specs=[
            pl.BlockSpec(memory_space=pltpu.SMEM),
            pl.BlockSpec((count, width), lambda i: (0, 0)),
            pl.BlockSpec((count, width), lambda i: (0, 0)),
            pl.BlockSpec((count, chunk), lambda i: (0, i)),
            pl.BlockSpec((count, chunk), lambda i: (0, i)),
        ],
        out_specs=[
            *[pl.BlockSpec((seqs, rows, chunk), lambda i: (0, 0, jnp.minimum(i, first_steps - 1)))]
            * sub,
            pl.BlockSpec(
                (tok_devices, 2, rows, PACK), lambda i: (0, jnp.maximum(i - first_steps, 0), 0, 0)
            ),
        ],
        out_shape=[
            *[jax.ShapeDtypeStruct((seqs, rows, ff - far * PACK), BF16)] * sub,
            jax.ShapeDtypeStruct((tok_devices, far, rows, PACK), BF16),
        ],
        scratch_shapes=[pltpu.VMEM((sub, seqs, rows, chunk), BF16)],
        compiler_params=pltpu.CompilerParams(vmem_limit_bytes=VMEM_LIMIT),
        cost_estimate=cost(
            flops=4 * count * width * ff,
            bytes_accessed=2 * width * ff + 4 * count * (width + ff),
            transcendentals=0,
        ),
        name="pair_grad_in",
    )(group, lhs, lhs_other, rhs, rhs_other)


def pair_grad_down(lhs, lhs_other, rhs, rhs_other, ff):
    count = lhs.shape[0]
    width = rhs.shape[1] - ff
    half = width // 2
    chunk = 768
    down = ff // chunk

    def body(l1_ref, l2_ref, r1_ref, r2_ref, out_ref):
        out = dot(l1_ref[...], r1_ref[...], TN) + dot(l2_ref[...], r2_ref[...], TN)
        out_ref[...] = out.astype(BF16)

    left = pl.BlockSpec((count, chunk), lambda i: (0, 1 + i))
    right = pl.BlockSpec((count, half), lambda i: (0, ff // half + jnp.where(i < down, 0, 1)))
    return pl.pallas_call(
        body,
        grid=(down + 1,),
        in_specs=[left, left, right, right],
        out_specs=pl.BlockSpec((chunk, half), lambda i: (i, 0)),
        out_shape=jax.ShapeDtypeStruct((ff + width, half), BF16),
        compiler_params=pltpu.CompilerParams(vmem_limit_bytes=VMEM_LIMIT),
        cost_estimate=cost(
            flops=4 * count * half * (ff + width),
            bytes_accessed=(ff + width) * (width + 4 * count) + 8 * count * width,
            transcendentals=0,
        ),
        name="pair_grad_down",
    )(lhs, lhs_other, rhs, rhs_other)


def input_grad(layer, group, ga, back, w_qkv):
    sub = len(back)
    cols, count = back[0].shape
    width = ga.shape[1]

    def body(group_ref, ga_ref, w_ref, *refs):
        back_refs, out_ref, acc_ref = refs[:sub], refs[sub], refs[sub + 1]
        step = pl.program_id(0)

        @pl.when(step == 0)
        def _():
            acc_ref[...] = jnp.zeros_like(acc_ref)

        for r in range(sub):

            @pl.when(step == r)
            def _():
                acc_ref[...] += dot(w_ref[0, 0], back_refs[r][...], NN)

        @pl.when(step == sub - 1)
        def _():
            out_ref[...] = ga_ref[...] + acc_ref[...].T

    return pl.pallas_call(
        body,
        grid_spec=pltpu.PrefetchScalarGridSpec(
            num_scalar_prefetch=1,
            grid=(sub,),
            in_specs=[
                pl.BlockSpec((count, width), lambda i, g: (0, 0)),
                pl.BlockSpec(
                    (1, 1, width, cols), lambda i, g: (layer, jnp.bitwise_xor(g[0], i), 0, 0)
                ),
                *[pl.BlockSpec((cols, count), lambda i, g: (0, 0))] * sub,
            ],
            out_specs=pl.BlockSpec((count, width), lambda i, g: (0, 0)),
            scratch_shapes=[pltpu.VMEM((width, count), F32)],
        ),
        out_shape=jax.ShapeDtypeStruct((count, width), F32),
        compiler_params=pltpu.CompilerParams(vmem_limit_bytes=VMEM_LIMIT),
        cost_estimate=cost(
            flops=2 * count * width * cols * sub,
            bytes_accessed=2 * sub * cols * (width + count) + 8 * count * width,
            transcendentals=0,
        ),
        name="input_grad",
    )(group, ga, w_qkv, *back)


def project(layer, group, parts, w_qkv):
    sub = len(parts)
    count = parts[0].shape[0]
    width, cols = w_qkv.shape[2:]

    def body(group_ref, w_ref, *refs):
        out_ref = refs[sub]
        for r in range(sub):
            out_ref[r * count : r * count + count, :] = dot(
                refs[r][...], w_ref[0, 0], NN
            ).astype(BF16)

    return pl.pallas_call(
        body,
        grid_spec=pltpu.PrefetchScalarGridSpec(
            num_scalar_prefetch=1,
            grid=(1,),
            in_specs=[
                pl.BlockSpec((1, 1, width, cols), lambda i, g: (layer, g[0], 0, 0)),
                *[pl.BlockSpec((count, width), lambda i, g: (0, 0))] * sub,
            ],
            out_specs=pl.BlockSpec((sub * count, cols), lambda i, g: (0, 0)),
        ),
        out_shape=jax.ShapeDtypeStruct((sub * count, cols), BF16),
        compiler_params=pltpu.CompilerParams(vmem_limit_bytes=VMEM_LIMIT),
        cost_estimate=cost(
            flops=2 * sub * count * width * cols,
            bytes_accessed=2 * (width * cols + sub * count * (width + cols)),
            transcendentals=0,
        ),
        name="project",
    )(group, w_qkv, *parts)


def qkv_grad(parts, grads, width, tok_devices, dp_devices):
    sub = len(parts)
    count = parts[0].shape[0]
    cols = grads[0].shape[0]
    rows = width // tok_devices
    few = rows // dp_devices

    def body(*refs):
        out_ref = refs[2 * sub]
        acc = jnp.zeros((cols, width), F32)
        for r in range(sub):
            acc += dot(refs[sub + r][...], refs[r][...], NN)
        acc = acc.T
        for t in range(tok_devices):
            for q in range(dp_devices):
                first = t * rows + q * few
                out_ref[q, t] = acc[first : first + few].astype(BF16)

    return pl.pallas_call(
        body,
        grid=(1,),
        in_specs=[
            *[pl.BlockSpec((count, width), lambda i: (0, 0))] * sub,
            *[pl.BlockSpec((cols, count), lambda i: (0, 0))] * sub,
        ],
        out_specs=pl.BlockSpec((dp_devices, tok_devices, few, cols), lambda i: (0, 0, 0, 0)),
        out_shape=jax.ShapeDtypeStruct((dp_devices, tok_devices, few, cols), BF16),
        compiler_params=pltpu.CompilerParams(vmem_limit_bytes=VMEM_LIMIT),
        cost_estimate=cost(
            flops=2 * sub * count * width * cols,
            bytes_accessed=2 * (width * cols + sub * count * (width + cols)),
            transcendentals=0,
        ),
        name="qkv_grad",
    )(*parts, *grads)


def attend_forward(qkv, far_dist, slopes, sub):
    length, width = qkv.shape
    cols = width // 3
    heads = cols // HEAD_DIM
    count = length // sub
    block = 256
    per = count // block

    def body(slope_ref, qkv_ref, dist_ref, *refs):
        ctx_refs, lse_ref, held_ref = refs[:sub], refs[sub], refs[sub + 1]
        step = pl.program_id(0)
        at = pl.ds(pl.multiple_of(step * block, block), block)
        dist = dist_ref[...]
        for h in range(heads):
            q = qkv_ref[at, h * 64 : h * 64 + 64]
            k = qkv_ref[:, cols + h * 64 : cols + h * 64 + 64]
            v = qkv_ref[:, 2 * cols + h * 64 : 2 * cols + h * 64 + 64]
            s = dot(k, q, NT) * SCALE - dist * slope_ref[h]
            top = jnp.max(s, axis=0, keepdims=True)
            e = jnp.exp(s - top)
            total = jnp.sum(e, axis=0, keepdims=True)
            ctx = dot(v, e.astype(BF16), TN) / total
            held_ref[h * 64 : h * 64 + 64, :] = ctx.astype(BF16)
            lse_ref[h : h + 1, :] = top + jnp.log(total)
        for i in range(length // block):

            @pl.when(step == i)
            def _():
                first = i % per * block
                ctx_refs[i // per][:, first : first + block] = held_ref[...]

    return pl.pallas_call(
        body,
        grid=(length // block,),
        in_specs=[
            pl.BlockSpec(memory_space=pltpu.SMEM),
            pl.BlockSpec((length, width), lambda i: (0, 0)),
            pl.BlockSpec((length, block), lambda i: (0, i)),
        ],
        out_specs=[
            *[pl.BlockSpec((cols, count), lambda i: (0, 0))] * sub,
            pl.BlockSpec((heads, block), lambda i: (0, i)),
        ],
        out_shape=[
            *[jax.ShapeDtypeStruct((cols, count), BF16)] * sub,
            jax.ShapeDtypeStruct((heads, length), F32),
        ],
        scratch_shapes=[pltpu.VMEM((cols, block), BF16)],
        compiler_params=pltpu.CompilerParams(vmem_limit_bytes=VMEM_LIMIT),
        cost_estimate=cost(
            flops=16 * heads * length * length * HEAD_DIM,
            bytes_accessed=4 * length * length,
            transcendentals=heads * length * length,
        ),
        name="attend_forward",
    )(slopes, qkv, far_dist)


def attend_backward(qkv, ctx, ctx_grad, lse, far_dist, slopes):
    length, width = qkv.shape
    sub = len(ctx)
    cols = width // 3
    heads = cols // HEAD_DIM
    count = length // sub
    block = 256
    per = count // block

    def body(slope_ref, qkv_ref, lse_ref, dist_ref, *refs):
        ctx_refs, g_refs, out_refs = refs[:sub], refs[sub : 2 * sub], refs[2 * sub : 3 * sub]
        dk_ref, dv_ref, dq_ref, held_ref, inner_ref = refs[3 * sub :]
        step = pl.program_id(0)
        at = pl.ds(pl.multiple_of(step * block, block), block)

        @pl.when(step == 0)
        def _():
            dk_ref[...] = jnp.zeros_like(dk_ref)
            dv_ref[...] = jnp.zeros_like(dv_ref)
            for r in range(sub):
                g = g_refs[r][...]
                both = g.astype(F32) * ctx_refs[r][...].astype(F32)
                for p in range(per):
                    of = slice(p * block, p * block + block)
                    held_ref[r * per + p] = g[:, of]
                    for h in range(heads):
                        inner_ref[r * per + p, h : h + 1, :] = jnp.sum(
                            both[h * 64 : h * 64 + 64, of], axis=0, keepdims=True
                        )

        dist = dist_ref[...]
        for h in range(heads):
            mine = slice(h * 64, h * 64 + 64)
            q = qkv_ref[at, mine]
            k = qkv_ref[:, cols + h * 64 : cols + h * 64 + 64]
            v = qkv_ref[:, 2 * cols + h * 64 : 2 * cols + h * 64 + 64]
            g = held_ref[step, mine, :]
            s = dot(k, q, NT) * SCALE - dist * slope_ref[h]
            p = jnp.exp(s - lse_ref[h : h + 1, :])
            gp = dot(v, g, NN)
            gs = (p * (gp - inner_ref[step, h : h + 1, :])).astype(BF16)
            dv_ref[:, mine] += dot(p.astype(BF16), g, NT)
            dk_ref[:, mine] += dot(gs, q, NN)
            dq_ref[step, mine, :] = (dot(k, gs, TN) * SCALE).astype(BF16)

        @pl.when(step == pl.num_programs(0) - 1)
        def _():
            for r in range(sub):
                of = slice(r * count, r * count + count)
                for p in range(per):
                    out_refs[r][:cols, p * block : p * block + block] = dq_ref[r * per + p]
                out_refs[r][cols : 2 * cols, :] = (dk_ref[of, :] * SCALE).T.astype(BF16)
                out_refs[r][2 * cols :, :] = dv_ref[of, :].T.astype(BF16)

    return pl.pallas_call(
        body,
        grid=(length // block,),
        in_specs=[
            pl.BlockSpec(memory_space=pltpu.SMEM),
            pl.BlockSpec((length, width), lambda i: (0, 0)),
            pl.BlockSpec((heads, block), lambda i: (0, i)),
            pl.BlockSpec((length, block), lambda i: (0, i)),
            *[pl.BlockSpec((cols, count), lambda i: (0, 0))] * (2 * sub),
        ],
        out_specs=[pl.BlockSpec((width, count), lambda i: (0, 0))] * sub,
        out_shape=[jax.ShapeDtypeStruct((width, count), BF16)] * sub,
        scratch_shapes=[
            pltpu.VMEM((length, cols), F32),
            pltpu.VMEM((length, cols), F32),
            pltpu.VMEM((length // block, cols, block), BF16),
            pltpu.VMEM((length // block, cols, block), BF16),
            pltpu.VMEM((length // block, heads, block), F32),
        ],
        compiler_params=pltpu.CompilerParams(vmem_limit_bytes=VMEM_LIMIT),
        cost_estimate=cost(
            flops=20 * heads * length * length * HEAD_DIM,
            bytes_accessed=4 * length * length,
            transcendentals=heads * length * length,
        ),
        name="attend_backward",
    )(slopes, qkv, lse, far_dist, *ctx, *ctx_grad)


def pack_columns(*values):
    parts = []
    for value in values:
        parts += [value[..., i : i + PACK] for i in range(0, value.shape[-1], PACK)]
    return jnp.concatenate(parts, axis=-2)


def unpack_plan(width, ff, tok_devices, dp_devices):
    far = dp_devices // 2
    half = width // 2
    row_out, row_down = width // tok_devices, ff // tok_devices
    plan = []
    for device in range(dp_devices):
        at, core = device // 2, device % 2
        pieces = []
        first_cols = ff - far * PACK
        for i in range(0, first_cols // far, PACK):
            pieces.append((2, 0, core * ff + at * (first_cols // far) + i, row_out))
        pieces.append((3, at * (row_down // far), core * half, row_down // far))
        pieces.append((1, at * (row_out // far), core * half, row_out // far))
        pieces.append((2, 0, core * ff + first_cols + at * PACK, row_out))
        for i in range(0, 3 * width, PACK):
            pieces.append((0, device * (row_out // dp_devices), i, row_out // dp_devices))
        plan.append(pieces)
    return plan


def assemble(packed, width, ff, tok_devices, dp_devices):
    row_out, row_down = width // tok_devices, ff // tok_devices
    plan = unpack_plan(width, ff, tok_devices, dp_devices)
    shapes = [
        (row_out, LAYERS, 3 * width),
        (row_out, LAYERS, width),
        (row_out, LAYERS, 2 * ff),
        (row_down, LAYERS, width),
    ]
    if row_out // dp_devices % 8:
        outs = [jnp.zeros(shape, F32) for shape in shapes]
        for layer in range(LAYERS):
            for device in range(dp_devices):
                row = 0
                for out, to_row, to_col, count in plan[device]:
                    piece = packed[layer][device, row : row + count].astype(F32)
                    outs[out] = (
                        outs[out].at[to_row : to_row + count, layer, to_col : to_col + PACK]
                    ).set(piece)
                    row += count
        return outs

    def body(*refs):
        in_refs, out_refs = refs[:LAYERS], refs[LAYERS:]
        for layer in range(LAYERS):
            for device in range(dp_devices):
                row = 0
                for out, to_row, to_col, count in plan[device]:
                    piece = in_refs[layer][device, row : row + count, :].astype(F32)
                    out_refs[out][
                        to_row : to_row + count, layer, to_col : to_col + PACK
                    ] = piece
                    row += count

    return pl.pallas_call(
        body,
        out_shape=[jax.ShapeDtypeStruct(shape, F32) for shape in shapes],
        compiler_params=pltpu.CompilerParams(vmem_limit_bytes=VMEM_LIMIT),
        name="assemble",
    )(*packed)


def swap(value, axis, bit):
    return lax.ppermute(value, axis, [(i, i ^ (1 << bit)) for i in range(lax.axis_size(axis))])


def bit_of(axis, bit):
    return (lax.axis_index(axis) >> bit) & 1


def bits_of(axis):
    return lax.axis_size(axis).bit_length() - 1


def add_up(*values):
    total = values[0].astype(F32)
    for value in values[1:]:
        total = total + value.astype(F32)
    return total.astype(BF16)


def reduce_half(value, axis, bit, dim):
    mine = bit_of(axis, bit)
    half = value.shape[dim] // 2
    kept = lax.dynamic_slice_in_dim(value, mine * half, half, dim)
    sent = lax.dynamic_slice_in_dim(value, (1 - mine) * half, half, dim)
    return add_up(kept, swap(sent, axis, bit))


def gather_pair(value, axis, bit, dim):
    mine = bit_of(axis, bit)
    other = swap(value, axis, bit)
    low = jnp.where(mine == 0, value, other)
    high = jnp.where(mine == 0, other, value)
    return jnp.stack((low, high), axis=dim)


def pin(*values):
    return lax.optimization_barrier(values)


def gather_dp(value):
    value = value[None]
    for bit in reversed(range(bits_of("dp"))):
        value = gather_pair(value, "dp", bit, 1)
        value = value.reshape(-1, *value.shape[2:])
    return value


def far_bits(sub):
    return [bit for bit in reversed(range(bits_of("tok"))) if (1 << bit) >= sub]


def per_device(
    tokens, mask, segments, replacement, w_qkv, w_out, w_in, w_down, ln_gain, ln_bias, cotangent
):
    tok_devices = lax.axis_size("tok")
    dp_devices = lax.axis_size("dp")
    seq_count, local_len, width = tokens.shape
    ff = w_down.shape[0]
    sub = tok_devices // seq_count
    per_group = HEADS // sub
    cols = per_group * HEAD_DIM
    tok_count = seq_count * local_len
    full_len = local_len * tok_devices
    tok_place = lax.axis_index("tok")
    group = tok_place % sub
    place_of = group.reshape(1)
    core = bit_of("dp", 0).reshape(1)
    near = [[j + sub * k for j in range(sub)] for k in range(seq_count)]

    def regroup(value):
        place = tok_place // sub
        parts = [lax.dynamic_index_in_dim(value, place, 0, False)]
        for r in range(1, seq_count):
            part = lax.dynamic_index_in_dim(value, place ^ r, 0, False)
            to = [(i, i ^ (r * sub)) for i in range(tok_devices)]
            parts.append(lax.ppermute(part, "tok", to))
        if seq_count == 2:
            low = jnp.where(place == 0, parts[0], parts[1])
            return jnp.stack((low, jnp.where(place == 0, parts[1], parts[0])))
        return jnp.stack(parts)[jnp.arange(seq_count) ^ place]

    def spread(value):
        return lax.all_to_all(value, "tok", 0, 0, axis_index_groups=near)

    near_pairs = [[(i, i ^ r) for i in range(tok_devices)] for r in range(1, sub)]

    def deal(parts):
        return [
            parts[0],
            *(lax.ppermute(p, "tok", to) for p, to in zip(parts[1:], near_pairs)),
        ]

    extra = jnp.zeros((seq_count, local_len, LANES), BF16)
    extra = extra.at[:, :, 0].set((mask == 1).astype(BF16))
    extra = extra.at[:, :, 1].set(segments.astype(BF16))
    mixed = regroup(jnp.concatenate((tokens, extra), axis=-1)).reshape(tok_count, -1)
    wq = split_layers_by_group(w_qkv, sub)
    wo = split_layers(w_out)
    mixed, wq, wo = pin(mixed, wq, wo)
    flags = mixed[:, width:]
    masked = flags[:, :1] == 1.0
    current = jnp.where(masked, replacement[None, :], mixed[:, :width].astype(F32))
    flat_in = current.astype(BF16)

    wi = split_layers(w_in)
    wd = split_layers(w_down)
    slopes = lax.dynamic_slice_in_dim(alibi_slopes(HEADS), group * per_group, per_group, 0)
    order = jnp.arange(sub, dtype=jnp.int32) ^ group
    place = (
        (jnp.arange(seq_count, dtype=jnp.int32)[None, :, None] * sub + order[:, None, None])
        * local_len
        + jnp.arange(local_len, dtype=jnp.int32)[None, None, :]
    ).reshape(full_len)
    far_dist = None
    stored = []
    for layer in range(LAYERS):
        sent = jnp.concatenate((flat_in, flags), axis=-1) if layer == 0 else flat_in
        parts = deal([sent] * sub)
        if layer == 0:
            *parts, wi = pin(*parts, wi)
            labels = jnp.concatenate([p[:, width + 1] for p in parts]).astype(F32)
            far_dist = jnp.where(
                labels[:, None] == labels[None, :],
                jnp.abs(place[:, None] - place[None, :]).astype(F32),
                FAR,
            )
        else:
            *parts, stored[0]["lhs_other"] = pin(*parts, stored[0]["lhs_other"])
        qkv = project(layer, place_of, parts, wq)
        *ctx_here, lse = attend_forward(qkv, far_dist, slopes, sub)
        ctx = deal(ctx_here)
        if layer == 0:
            *ctx, wd = pin(*ctx, wd)
        else:
            *ctx, cot = pin(*ctx, regroup(cotangent))
        lhs, a, b, summed, z, current, flat_in = feed_forward(
            layer, place_of, current, ctx, wo, wi, wd, ln_gain, ln_bias
        )
        stored.append(
            {
                "attend": (parts, qkv, ctx_here, lse),
                "feed": (z, summed, a, b),
                "lhs": lhs,
                "lhs_other": swap(lhs, "dp", 0),
            }
        )
    layer_out = flat_in.reshape(seq_count, local_len, width)
    gradient = cot.reshape(tok_count, width).astype(F32)
    small = []
    row_out = width // tok_devices
    row_down = ff // tok_devices
    half = width // 2
    x_bits = list(reversed(range(1, bits_of("dp"))))
    far = dp_devices // 2

    def near_sum(parts):
        return add_up(*deal(parts))

    def x_sum_rows(arrays):
        for bit in x_bits:
            at = bit_of("dp", bit)
            picked = []
            for choice in (at, 1 - at):
                picked.append(
                    jnp.concatenate(
                        [
                            lax.dynamic_slice_in_dim(
                                v, choice * (v.shape[1] // 2), v.shape[1] // 2, 1
                            )
                            for v in arrays
                        ],
                        axis=1,
                    )
                )
            total = add_up(picked[0], swap(picked[1], "dp", bit))
            ends = [v.shape[1] // 2 for v in arrays]
            arrays = []
            for end in ends:
                first = sum(v.shape[1] for v in arrays)
                arrays.append(total[:, first : first + end])
        return total

    def x_sum_columns(value):
        for bit in x_bits:
            value = reduce_half(value, "dp", bit, value.ndim - 1)
        return value

    def far_sum(value):
        for bit in far_bits(sub):
            value = reduce_half(value, "tok", bit, 0)
        return value[0]

    def by_place(value):
        return value.reshape(seq_count, sub, *value.shape[1:]).swapaxes(0, 1)

    def spread_sum(value):
        return add_up(*spread(by_place(value)))

    def deal_sum(value):
        value = by_place(value)
        return near_sum(
            [lax.dynamic_index_in_dim(value, group ^ r, 0, False) for r in range(sub)]
        )

    def dp_sum(value):
        value = add_up(*lax.all_to_all(value, "dp", 0, 0))
        return value.reshape(seq_count, sub, -1, 3 * cols)

    def by_head(value):
        value = spread(value.swapaxes(0, 1)).reshape(sub, seq_count, -1, 3, cols)
        return value.transpose(1, 2, 3, 0, 4).reshape(seq_count, -1, 3 * width)

    packed = [None] * LAYERS
    before = None
    for layer in reversed(range(LAYERS)):
        parts, qkv, ctx_here, lse = stored[layer]["attend"]
        z, summed, a, b = stored[layer]["feed"]
        lhs, lhs_other = stored[layer]["lhs"], stored[layer]["lhs_other"]
        mine, send, ga, small_part, *gctx = feed_backward(
            layer, core, place_of, gradient, z, summed, a, b, wo, wi, wd, ln_gain, sub
        )
        small.insert(0, small_part)
        if before is not None:
            mine, first, last, qkv_dp, layer_out = pin(
                mine,
                near_sum(before["first"]),
                x_sum_rows(before["rest"]),
                dp_sum(before["qkv"]),
                regroup(layer_out),
            )
            last = jnp.concatenate((before["down"], last), axis=1)
        other = swap(send, "dp", 0)
        ctx_grad = deal(gctx)
        g_down = pair_grad_down(lhs, lhs_other, mine, other, ff)
        *g_first, g_last = pair_grad_in(
            place_of, lhs, lhs_other, mine, other, ff, tok_devices, sub, far
        )
        done = (*ctx_grad, g_down, g_last, *g_first)
        if before is not None:
            done += (x_sum_columns(first), by_head(qkv_dp), last)
        done = pin(*done)
        ctx_grad, g_down, g_last = done[:sub], done[sub], done[sub + 1]
        g_first = done[sub + 2 : 2 * sub + 2]
        g_out = g_down[ff:].reshape(tok_devices, row_out, half)
        g_down = g_down[:ff].reshape(tok_devices, row_down, half)
        g_last = g_last.reshape(tok_devices, far * row_out, PACK)
        head_grad = attend_backward(qkv, ctx_here, ctx_grad, lse, far_dist, slopes)
        if before is not None:
            first, qkv_dp, last = done[2 * sub + 2 :]
            both = pin(
                *head_grad,
                spread_sum(last),
                near_sum(g_first),
                x_sum_rows((g_down, g_out, g_last)),
            )
            head_grad, (last, g_first, g_last) = both[:sub], both[sub:]
            g_qkv = dp_sum(qkv_grad(parts, head_grad, width, tok_devices, dp_devices))
            before_all = pack_columns(first, last, qkv_dp)
            both = pin(
                *head_grad, g_qkv, x_sum_columns(g_first), deal_sum(g_last), far_sum(before_all)
            )
            head_grad, (g_qkv, g_first, g_last, before_all) = both[:sub], both[sub:]
            packed[layer + 1] = lax.all_gather(before_all, "dp")
            back = deal(head_grad)
            packed[layer] = gather_dp(far_sum(pack_columns(g_first, g_last, by_head(g_qkv))))
        else:
            g_qkv = qkv_grad(parts, head_grad, width, tok_devices, dp_devices)
            both = pin(*deal(head_grad), g_qkv, x_sum_rows((g_down,)), g_out, g_last, *g_first)
            back, (g_qkv, g_down, g_out, g_last) = both[:sub], both[sub : sub + 4]
            before = {
                "first": both[sub + 4 :],
                "down": g_down,
                "rest": (g_out, g_last),
                "qkv": g_qkv,
            }
        gradient = input_grad(layer, place_of, ga, back, wq)
    grad_tokens = jnp.where(masked, 0.0, gradient).astype(BF16)
    grad_tokens = regroup(grad_tokens.reshape(seq_count, local_len, width)).astype(F32)
    small.append(jnp.sum(jnp.where(masked, gradient, 0.0), axis=0, keepdims=True))
    small = jnp.concatenate(small, axis=0).reshape(-1, tok_devices, row_out).transpose(1, 0, 2)
    small = jnp.sum(lax.all_to_all(small, "tok", 0, 0), axis=0)
    for bit in range(bits_of("dp")):
        small = small + swap(small, "dp", bit)
    by_layer = small[: 4 * LAYERS].reshape(LAYERS, 2, 2, row_out)
    return (
        layer_out,
        grad_tokens,
        small[-1],
        *assemble(packed, width, ff, tok_devices, dp_devices),
        by_layer[:, 0],
        by_layer[:, 1],
    )


def solution(mesh):
    in_specs = (
        P("dp", "tok", None),
        P("dp", "tok"),
        P("dp", "tok"),
        P(),
        P(),
        P(),
        P(),
        P(),
        P(),
        P(),
        P("dp", "tok", None),
    )
    out_specs = (
        P("dp", "tok", None),
        P("dp", "tok", None),
        P("tok"),
        P("tok", None, None),
        P("tok", None, None),
        P("tok", None, None),
        P("tok", None, None),
        P(None, None, "tok"),
        P(None, None, "tok"),
    )
    return jax.shard_map(
        per_device, mesh=mesh, in_specs=in_specs, out_specs=out_specs, check_vma=False
    )
```

time: 839 us -> 546 us (0.65)
  blocking collectives: 125 us -> 0 us
  Pallas kernels: 90.1 us -> 211 us
  local copies, waits for them, and re-layouts: 131 us -> 29.7 us
  matrix products: 98 us -> 0 us
  other arithmetic: 87.6 us -> 35.6 us
  starting transfers between devices: 109 us -> 78.8 us
    ppermute x40 -> x15, waiting for transfers between devices: 165 us -> 24.3 us  [swap(): lax.ppermute(value, axis, [(i, i ^ 1 << bit) for i in range(lax.axis_size...]
    pallas_call x0 -> x16, Pallas kernels: none -> 129 us  [the longest x2 29.1 us: feed_backward(): pl.pallas_call(body, grid=(steps,), in_specs=[pl.BlockSpec(memory_space=p...]
    ppermute x0 -> x37, waiting for transfers between devices: none -> 120 us  [the longest x33 95.9 us: deal(): lax.ppermute(p, 'tok', to)]
    dot_general x24 -> x0, matrix products: 98 us -> none  [dot(): return lax.dot_general(a, b, (dims, ((), ())), preferred_element_type=F32)]
    all_gather x1 -> x0, blocking collectives: 76 us -> none  [per_device(): small = lax.all_gather(jnp.stack(small, axis=0), ('dp', 'tok'))]
    all_to_all x3 -> x0, blocking collectives: 49.1 us -> none  [the longest x2 30.9 us: spread(): return lax.all_to_all(value, 'tok', 0, 0, axis_index_groups=near)]
    ppermute x0 -> x37, starting transfers between devices: none -> 44.7 us  [the longest x33 37.5 us: deal(): lax.ppermute(p, 'tok', to)]
    ppermute x40 -> x15, starting transfers between devices: 52.9 us -> 11.3 us  [swap(): lax.ppermute(value, axis, [(i, i ^ 1 << bit) for i in range(lax.axis_size...]
  transfers between devices with their start and end apart: 55 -> 59, of which waited for: 22 -> 28; matrix products, arithmetic and copies ran while one was open for 28% -> 7% of each run, Pallas kernels for 8% -> 27%
where the time goes in v2:
time: 546 us; the launch traced here: 536 us
  Pallas kernels  211 us (39%)
  waiting for transfers between devices  165 us (30%)
  starting transfers between devices  78.8 us (14%)
  other arithmetic  35.6 us (7%)
  local copies, waits for them, and re-layouts  29.7 us (5%)
  between operations  15.6 us (3%)
    ppermute x33, waiting for transfers between devices, deal(): lax.ppermute(p, 'tok', to)  95.9 us
    ppermute x33, starting transfers between devices, deal(): lax.ppermute(p, 'tok', to)  37.5 us
    pallas_call x3, Pallas kernels, split_layers(): pl.pallas_call(body, grid=(rows // row_block, cols // col_block), in_spec...  33.8 us
    pallas_call x2, Pallas kernels, feed_backward(): pl.pallas_call(body, grid=(steps,), in_specs=[pl.BlockSpec(memory_space=p...  29.1 us
    pallas_call x2, Pallas kernels, feed_forward(): pl.pallas_call(body, grid=(steps,), in_specs=[pl.BlockSpec(memory_space=p...  27 us
    pallas_call x2, Pallas kernels, attend_backward(): pl.pallas_call(body, grid=(length // block,), in_specs=[pl.BlockSpec(memo...  25.3 us
    ppermute x4, waiting for transfers between devices, regroup(): parts.append(lax.ppermute(part, 'tok', to))  24.5 us
    ppermute x15, waiting for transfers between devices, swap(): lax.ppermute(value, axis, [(i, i ^ 1 << bit) for i in range(lax.axis_size...  24.3 us
  transfers between devices with their start and end apart: 59, of which 28 were waited for; matrix products, arithmetic and copies ran while one was open for 7% of the time, Pallas kernels for 27%

profile of v2, /device:TPU:0, one launch (start us, length us, event | category | flops | bytes accessed | tf_op | source)
XLA Modules:
  0.0 535.6 jit_solution(2020547838912473823)
XLA Ops:
  13.8 8.5 %split_qkv.1.w_ref = bf16[2,4,768,576]{3,2,1,0:T(8,128)(2,1)} custom-call(bf16[768,2,2304]{2,1,0:T(2,128)(2,1)} %in_ref.4), custom_call_target="tpu_custom_call" | custom-call | flops 7247757312 | bytes 14155776 | tf_op jit(solution)/shard_map/split_qkv/pallas_call | solution.py:97
  22.3 16.2 %split_layers.4.refs_6_.refs_7_.wg_ref.wu_ref = bf16[2,768,6144]{2,1,0:T(8,128)(2,1)} custom-call(bf16[768,2,6144]{2,1,0:T(2,128)(2,1)} %in_ref.6), custom_call_target="tpu_custom_call" | custom-call | flops 19327352832 | bytes 37748736 | tf_op jit(solution)/shard_map/split_layers/pallas_call | solution.py:62
  38.5 13.0 %split_layers.5.refs_8_.wd_ref = bf16[2,3072,768]{2,1,0:T(8,128)(2,1)} custom-call(bf16[3072,2,768]{2,1,0:T(2,128)(2,1)} %in_ref.7), custom_call_target="tpu_custom_call" | custom-call | flops 9663676416 | bytes 18874368 | tf_op jit(solution)/shard_map/split_layers/pallas_call | solution.py:62
  61.4 8.3 %collective-permute-done.1.refs_1_ = bf16[256,896]{1,0:T(8,128)(2,1)S(1)} collective-permute-done((bf16[256,896]{1,0:T(8,128)(2,1)S(1)}, bf16[256,896]{1,0:T(8,128)(2,1)S(1)}, u32[]{:S(2)}, u32[]{:S(2)}) %collective-permute-start.1) | collective-permute-done | bytes 458784 | tf_op jit(solution)/shard_map/ppermute | solution.py:841
  72.1 7.9 %collective-permute-done.3.refs_3_ = bf16[256,896]{1,0:T(8,128)(2,1)S(1)} collective-permute-done((bf16[256,896]{1,0:T(8,128)(2,1)S(1)}, bf16[256,896]{1,0:T(8,128)(2,1)S(1)}, u32[]{:S(2)}, u32[]{:S(2)}) %collective-permute-start.3) | collective-permute-done | bytes 458784 | tf_op jit(solution)/shard_map/ppermute | solution.py:841
  87.7 11.3 %attend_forward.2 = (bf16[192,256]{1,0:T(8,128)(2,1)}, bf16[192,256]{1,0:T(8,128)(2,1)}, bf16[192,256]{1,0:T(8,128)(2,1)}, bf16[192,256]{1,0:T(8,128)(2,1)}, f32[3,1024]{1,0:T(4,128)}) custom-call(f32[3]{0:T(128)} %dynamic_slice.94.slope_ref, bf16[1024,576]{1,0:T(8,128)(2,1)} %project.2.qkv_ref, f32[1024,1024]{1,0:T(8,128)} %convert_select_fusion.dist_ref), custom_call_target="tpu_custom_call" | custom-call | flops 12884901888 | bytes 4194304 | tf_op jit(solution)/shard_map/attend_forward/pallas_call | solution.py:573
  108.4 13.8 %feed_forward.2 = (bf16[256,4608]{1,0:T(8,128)(2,1)}, bf16[256,3072]{1,0:T(8,128)(2,1)}, bf16[256,3072]{1,0:T(8,128)(2,1)}, f32[256,768]{1,0:T(8,128)}, f32[256,...) custom-call(s32[1]{0:T(128)} %bitcast.1.group_ref, bf16[192,256]{1,0:T(8,128)(2,1)} %get-tuple-element.182.refs_0_, ...), custom_call_target="tpu_custom_call" | custom-call | flops 15703474176 | bytes 23986176 | tf_op jit(solution)/shard_map/feed_forward/pallas_call | solution.py:185
  126.2 8.6 %collective-permute-done.14 = bf16[128,768]{1,0:T(8,128)(2,1)S(1)} collective-permute-done((bf16[128,768]{1,0:T(8,128)(2,1)S(1)}, bf16[128,768]{1,0:T(8,128)(2,1)S(1)}, u32[]{:S(2)}, u32[]{:S(2)}) %collective-permute-start.14) | collective-permute-done | bytes 196640 | tf_op jit(solution)/shard_map/ppermute | solution.py:827
  139.7 7.9 %collective-permute-done.9.refs_3_ = bf16[256,768]{1,0:T(8,128)(2,1)} collective-permute-done((bf16[256,768]{1,0:T(8,128)(2,1)}, bf16[256,768]{1,0:T(8,128)(2,1)}, u32[]{:S(2)}, u32[]{:S(2)}) %collective-permute-start.9) | collective-permute-done | bytes 393248 | tf_op jit(solution)/shard_map/ppermute | solution.py:841
  152.5 11.3 %attend_forward.3 = (bf16[192,256]{1,0:T(8,128)(2,1)}, bf16[192,256]{1,0:T(8,128)(2,1)}, bf16[192,256]{1,0:T(8,128)(2,1)}, bf16[192,256]{1,0:T(8,128)(2,1)}, f32[3,1024]{1,0:T(4,128)}) custom-call(f32[3]{0:T(128)} %dynamic_slice.94.slope_ref, bf16[1024,576]{1,0:T(8,128)(2,1)} %project.3.qkv_ref, f32[1024,1024]{1,0:T(8,128)} %convert_select_fusion.dist_ref), custom_call_target="tpu_custom_call" | custom-call | flops 12884901888 | bytes 4194304 | tf_op jit(solution)/shard_map/attend_forward/pallas_call | solution.py:573
  172.2 13.2 %feed_forward.3 = (bf16[256,4608]{1,0:T(8,128)(2,1)}, bf16[256,3072]{1,0:T(8,128)(2,1)}, bf16[256,3072]{1,0:T(8,128)(2,1)}, f32[256,768]{1,0:T(8,128)}, f32[256,...) custom-call(s32[1]{0:T(128)} %bitcast.1.group_ref, bf16[192,256]{1,0:T(8,128)(2,1)} %get-tuple-element.200.refs_0_, ...), custom_call_target="tpu_custom_call" | custom-call | flops 15703474176 | bytes 23986176 | tf_op jit(solution)/shard_map/feed_forward/pallas_call | solution.py:185
  185.5 14.6 %feed_backward.2 = (bf16[256,3840]{1,0:T(8,128)(2,1)}, bf16[256,3840]{1,0:T(8,128)(2,1)}, f32[256,768]{1,0:T(8,128)}, f32[4,768]{1,0:T(4,128)}, bf16[192,256]{1,...) custom-call(s32[1]{0:T(128)} %bitcast.core_ref, ...), custom_call_target="tpu_custom_call" | custom-call | flops 15703474176 | bytes 26345472 | tf_op jit(solution)/shard_map/feed_backward/pallas_call | solution.py:287
  204.5 8.2 %collective-permute-done.28 = bf16[128,768]{1,0:T(8,128)(2,1)S(1)} collective-permute-done((bf16[128,768]{1,0:T(8,128)(2,1)S(1)}, bf16[128,768]{1,0:T(8,128)(2,1)S(1)}, u32[]{:S(2)}, u32[]{:S(2)}) %collective-permute-start.28) | collective-permute-done | bytes 196640 | tf_op jit(solution)/shard_map/ppermute | solution.py:827
  214.8 7.4 %pair_grad_in.2 = (bf16[2,96,2304]{2,1,0:T(8,128)(2,1)}, bf16[2,96,2304]{2,1,0:T(8,128)(2,1)}, bf16[2,96,2304]{2,1,0:T(8,128)(2,1)}, bf16[2,96,2304]{2,1,0:T(8,128)(2,1)}, bf16[8,2,96,384]{3,2,1,0:T(8,128)(2,1)}) custom-call(s32[1]{0:T(128)} %bitcast.1.group_ref, bf16[256,4608]{1,0:T(8,128)(2,1)} %get-tuple-element.215.l1_ref, bf16[256,4608]{1,0:T(8,128)(2,1)} %copy-done.29, ...), custom_call_target="tpu_custom_call" | custom-call | flops 9663676416 | bytes 8650752 | tf_op jit(solution)/shard_map/pair_grad_in/pallas_call | solution.py:361
  232.6 12.7 %attend_backward.2 = (bf16[576,256]{1,0:T(8,128)(2,1)}, bf16[576,256]{1,0:T(8,128)(2,1)}, bf16[576,256]{1,0:T(8,128)(2,1)}, bf16[576,256]{1,0:T(8,128)(2,1)}) custom-call(f32[3]{0:T(128)} %dynamic_slice.94.slope_ref, bf16[1024,576]{1,0:T(8,128)(2,1)} %project.3.qkv_ref, f32[3,1024]{1,0:T(4,128)} %get-tuple-element.210.lse_ref, ...), custom_call_target="tpu_custom_call" | custom-call | flops 16106127360 | bytes 4194304 | tf_op jit(solution)/shard_map/attend_backward/pallas_call | solution.py:654
  276.8 14.5 %feed_backward.3 = (bf16[256,3840]{1,0:T(8,128)(2,1)}, bf16[256,3840]{1,0:T(8,128)(2,1)}, f32[256,768]{1,0:T(8,128)}, f32[4,768]{1,0:T(4,128)}, bf16[192,256]{1,...) custom-call(s32[1]{0:T(128)} %bitcast.core_ref, ...), custom_call_target="tpu_custom_call" | custom-call | flops 15703474176 | bytes 26345472 | tf_op jit(solution)/shard_map/feed_backward/pallas_call | solution.py:287
  296.3 7.7 %collective-permute-done.26 = bf16[2,96,2304]{2,1,0:T(8,128)(2,1)} collective-permute-done((bf16[2,96,2304]{2,1,0:T(8,128)(2,1)}, bf16[2,96,2304]{2,1,0:T(8,128)(2,1)}, u32[]{:S(2)}, u32[]{:S(2)}) %collective-permute-start.26) | collective-permute-done | bytes 884768 | tf_op jit(solution)/shard_map/ppermute | solution.py:841
  324.7 7.5 %pair_grad_in.3 = (bf16[2,96,2304]{2,1,0:T(8,128)(2,1)}, bf16[2,96,2304]{2,1,0:T(8,128)(2,1)}, bf16[2,96,2304]{2,1,0:T(8,128)(2,1)}, bf16[2,96,2304]{2,1,0:T(8,128)(2,1)}, bf16[8,2,96,384]{3,2,1,0:T(8,128)(2,1)}) custom-call(s32[1]{0:T(128)} %bitcast.1.group_ref, bf16[256,4608]{1,0:T(8,128)(2,1)} %get-tuple-element.190.l1_ref, bf16[256,4608]{1,0:T(8,128)(2,1)} %copy-done.28, ...), custom_call_target="tpu_custom_call" | custom-call | flops 9663676416 | bytes 8650752 | tf_op jit(solution)/shard_map/pair_grad_in/pallas_call | solution.py:361
  356.3 12.7 %attend_backward.3 = (bf16[576,256]{1,0:T(8,128)(2,1)}, bf16[576,256]{1,0:T(8,128)(2,1)}, bf16[576,256]{1,0:T(8,128)(2,1)}, bf16[576,256]{1,0:T(8,128)(2,1)}) custom-call(f32[3]{0:T(128)} %dynamic_slice.94.slope_ref, bf16[1024,576]{1,0:T(8,128)(2,1)} %project.2.qkv_ref, f32[3,1024]{1,0:T(4,128)} %get-tuple-element.256.lse_ref, ...), custom_call_target="tpu_custom_call" | custom-call | flops 16106127360 | bytes 4194304 | tf_op jit(solution)/shard_map/attend_backward/pallas_call | solution.py:654
  368.9 26.4 %collective-permute-done.34 = bf16[2,96,2304]{2,1,0:T(8,128)(2,1)} collective-permute-done((bf16[2,96,2304]{2,1,0:T(8,128)(2,1)}, bf16[2,96,2304]{2,1,0:T(8,128)(2,1)}, u32[]{:S(2)}, u32[]{:S(2)}) %collective-permute-start.34) | collective-permute-done | bytes 884768 | tf_op jit(solution)/shard_map/ppermute | solution.py:841
  426.0 10.9 %collective-permute-done.40 = bf16[2,336,384]{2,1,0:T(8,128)(2,1)} collective-permute-done((bf16[2,336,384]{2,1,0:T(8,128)(2,1)}, bf16[2,336,384]{2,1,0:T(8,128)(2,1)}, u32[]{:S(2)}, u32[]{:S(2)}) %collective-permute-start.40) | collective-permute-done | bytes 516128 | tf_op jit(solution)/shard_map/ppermute | solution.py:841
  464.9 16.7 %collective-permute-done.49 = bf16[1,768,384]{2,1,0:T(8,128)(2,1)S(1)} collective-permute-done((bf16[1,768,384]{2,1,0:T(8,128)(2,1)S(1)}, bf16[1,768,384]{2,1,0:T(8,128)(2,1)S(1)}, u32[]{:S(2)}, u32[]{:S(2)}) %collective-permute-start.49) | collective-permute-done | bytes 589856 | tf_op jit(solution)/shard_map/ppermute | solution.py:753
  508.6 7.8 %collective-permute-done.46 = bf16[128,768]{1,0:T(8,128)(2,1)S(1)} collective-permute-done((bf16[128,768]{1,0:T(8,128)(2,1)S(1)}, bf16[128,768]{1,0:T(8,128)(2,1)S(1)}, u32[]{:S(2)}, u32[]{:S(2)}) %collective-permute-start.46) | collective-permute-done | bytes 196640 | tf_op jit(solution)/shard_map/ppermute | solution.py:827
  519.6 8.7 %assemble.1 = (f32[96,2,2304]{2,1,0:T(2,128)}, f32[96,2,768]{2,1,0:T(2,128)}, f32[96,2,6144]{2,1,0:T(2,128)}, f32[384,2,768]{2,1,0:T(2,128)}) custom-call(bf16[4,768,384]{2,1,0:T(8,128)(2,1)} %bitcast.130, bf16[4,768,384]{2,1,0:T(8,128)(2,1)} %bitcast.139), custom_call_target="tpu_custom_call" | custom-call | tf_op jit(solution)/shard_map/assemble/pallas_call | solution.py:744
  (332 shorter events, 244.2 us)
Async XLA Ops:
  9.7 46.5 %collective-permute-start = (bf16[128,896]{1,0:T(8,128)(2,1)S(1)}, bf16[128,896]{1,0:T(8,128)(2,1)S(1)}, u32[]{:S(2)}, u32[]{:S(2)}) collective-permute-start(bf16[128,896]{1,0:T(8,128)(2,1)S(1)} %fusion.6), channel_id=1, source_target_pairs={{0,4},{1,5},{2,6},{3,7},{4,0},{5,1},{6,2},{7,3},{8,12},{9,13},{10,... | collective-permute-start | bytes 688136 | tf_op jit(solution)/shard_map/ppermute | solution.py:827
  122.2 25.3 %collective-permute-start.10 = (bf16[256,4608]{1,0:T(8,128)(2,1)}, bf16[256,4608]{1,0:T(8,128)(2,1)S(1)}, u32[]{:S(2)}, u32[]{:S(2)}) collective-permute-start(bf16[256,4608]{1,0:T(8,128)(2,1)} %get-tuple-element.190.l1_ref), channel_id=1, source_target_pairs={{0,8},{8,0},{16,24},{24,16},{1,9},{9,1},{17,25},{25,17},{2,10},{10... | collective-permute-start | bytes 7077896 | tf_op jit(solution)/shard_map/ppermute | solution.py:753
  124.4 23.2 %collective-permute-start.9 = (bf16[256,768]{1,0:T(8,128)(2,1)}, bf16[256,768]{1,0:T(8,128)(2,1)}, u32[]{:S(2)}, u32[]{:S(2)}) collective-permute-start(bf16[256,768]{1,0:T(8,128)(2,1)} %get-tuple-element.191.refs_0_), channel_id=1, source_target_pairs={{0,3},{1,2},{2,1},{3,0},{4,7},{5,6},{6,5},{7,4},{8,11},{9,10},{10,... | collective-permute-start | bytes 1179656 | tf_op jit(solution)/shard_map/ppermute | solution.py:841
  185.4 28.0 %collective-permute-start.18 = (bf16[256,4608]{1,0:T(8,128)(2,1)}, bf16[256,4608]{1,0:T(8,128)(2,1)S(1)}, u32[]{:S(2)}, u32[]{:S(2)}) collective-permute-start(bf16[256,4608]{1,0:T(8,128)(2,1)} %get-tuple-element.215.l1_ref), channel_id=1, source_target_pairs={{0,8},{8,0},{16,24},{24,16},{1,9},{9,1},{17,25},{25,17},{2,10},{10... | collective-permute-start | bytes 7077896 | tf_op jit(solution)/shard_map/ppermute | solution.py:753
  202.7 26.2 %collective-permute-start.15 = (bf16[192,256]{1,0:T(8,128)(2,1)}, bf16[192,256]{1,0:T(8,128)(2,1)S(1)}, u32[]{:S(2)}, u32[]{:S(2)}) collective-permute-start(bf16[192,256]{1,0:T(8,128)(2,1)} %get-tuple-element.212), channel_id=1, source_target_pairs={{0,1},{1,0},{2,3},{3,2},{4,5},{5,4},{6,7},{7,6},{8,9},{9,8},{10,11... | collective-permute-start | bytes 294920 | tf_op jit(solution)/shard_map/ppermute | solution.py:841
  204.2 24.7 %collective-permute-start.16 = (bf16[192,256]{1,0:T(8,128)(2,1)}, bf16[192,256]{1,0:T(8,128)(2,1)S(1)}, u32[]{:S(2)}, u32[]{:S(2)}) collective-permute-start(bf16[192,256]{1,0:T(8,128)(2,1)} %get-tuple-element.213), channel_id=1, source_target_pairs={{0,2},{1,3},{2,0},{3,1},{4,6},{5,7},{6,4},{7,5},{8,10},{9,11},{10,... | collective-permute-start | bytes 294920 | tf_op jit(solution)/shard_map/ppermute | solution.py:841
  231.1 27.1 %collective-permute-start.23 = (bf16[8,192,384]{2,1,0:T(8,128)(2,1)S(1)}, bf16[8,192,384]{2,1,0:T(8,128)(2,1)S(1)}, u32[]{:S(2)}, u32[]{:S(2)}) collective-permute-start(bf16[8,192,384]{2,1,0:T(8,128)(2,1)S(1)} %constant_dynamic-slice_fusion.14), channel_id=1, source_target_pairs={{0,16},{8,24},{16,0},{24,8},{1,17},{9,25},{17,1},{25,9},{2,18},{10... | collective-permute-start | bytes 3538952 | tf_op jit(solution)/shard_map/ppermute | solution.py:753
  263.6 30.3 %collective-permute-start.27 = (bf16[8,144,384]{2,1,0:T(8,128)(2,1)}, bf16[8,144,384]{2,1,0:T(8,128)(2,1)}, u32[]{:S(2)}, u32[]{:S(2)}) collective-permute-start(bf16[8,144,384]{2,1,0:T(8,128)(2,1)} %pad_maximum_fusion.3), channel_id=1, source_target_pairs={{0,16},{8,24},{16,0},{24,8},{1,17},{9,25},{17,1},{25,9},{2,18},{10... | collective-permute-start | bytes 2654216 | tf_op jit(solution)/shard_map/ppermute | solution.py:753
  264.3 32.0 %collective-permute-start.24 = (bf16[2,96,2304]{2,1,0:T(8,128)(2,1)}, bf16[2,96,2304]{2,1,0:T(8,128)(2,1)}, u32[]{:S(2)}, u32[]{:S(2)}) collective-permute-start(bf16[2,96,2304]{2,1,0:T(8,128)(2,1)} %get-tuple-element.247), channel_id=1, source_target_pairs={{0,1},{1,0},{2,3},{3,2},{4,5},{5,4},{6,7},{7,6},{8,9},{9,8},{10,11... | collective-permute-start | bytes 2654216 | tf_op jit(solution)/shard_map/ppermute | solution.py:841
  264.9 31.4 %collective-permute-start.25 = (bf16[2,96,2304]{2,1,0:T(8,128)(2,1)}, bf16[2,96,2304]{2,1,0:T(8,128)(2,1)}, u32[]{:S(2)}, u32[]{:S(2)}) collective-permute-start(bf16[2,96,2304]{2,1,0:T(8,128)(2,1)} %get-tuple-element.248), channel_id=1, source_target_pairs={{0,2},{1,3},{2,0},{3,1},{4,6},{5,7},{6,4},{7,5},{8,10},{9,11},{10,... | collective-permute-start | bytes 2654216 | tf_op jit(solution)/shard_map/ppermute | solution.py:841
  266.6 37.3 %collective-permute-start.26 = (bf16[2,96,2304]{2,1,0:T(8,128)(2,1)}, bf16[2,96,2304]{2,1,0:T(8,128)(2,1)}, u32[]{:S(2)}, u32[]{:S(2)}) collective-permute-start(bf16[2,96,2304]{2,1,0:T(8,128)(2,1)} %get-tuple-element.249), channel_id=1, source_target_pairs={{0,3},{1,2},{2,1},{3,0},{4,7},{5,6},{6,5},{7,4},{8,11},{9,10},{10,... | collective-permute-start | bytes 2654216 | tf_op jit(solution)/shard_map/ppermute | solution.py:841
  267.8 25.9 %all-to-all-start = ((bf16[4,8,24,576]{3,2,1,0:T(8,128)(2,1)}), bf16[4,8,24,576]{3,2,1,0:T(8,128)(2,1)S(1)}, u32[]{:S(2)}, u32[]{:S(2)}) async-start(bf16[4,8,24,576]{3,2,1,0:T(8,128)(2,1)} %qkv_grad.2), calls=%async_computation | async-start | bytes 1966080 | tf_op jit(solution)/shard_map/all_to_all | solution.py:957
  291.4 33.4 %collective-permute-start.32 = (bf16[256,3840]{1,0:T(8,128)(2,1)}, bf16[256,3840]{1,0:T(8,128)(2,1)}, u32[]{:S(2)}, u32[]{:S(2)}) collective-permute-start(bf16[256,3840]{1,0:T(8,128)(2,1)} %get-tuple-element.263), channel_id=1, source_target_pairs={{0,8},{8,0},{16,24},{24,16},{1,9},{9,1},{17,25},{25,17},{2,10},{10... | collective-permute-start | bytes 5898248 | tf_op jit(solution)/shard_map/ppermute | solution.py:753
  314.1 24.9 %collective-permute-start.29 = (bf16[192,256]{1,0:T(8,128)(2,1)}, bf16[192,256]{1,0:T(8,128)(2,1)}, u32[]{:S(2)}, u32[]{:S(2)}) collective-permute-start(bf16[192,256]{1,0:T(8,128)(2,1)} %get-tuple-element.258), channel_id=1, source_target_pairs={{0,1},{1,0},{2,3},{3,2},{4,5},{5,4},{6,7},{7,6},{8,9},{9,8},{10,11... | collective-permute-start | bytes 294920 | tf_op jit(solution)/shard_map/ppermute | solution.py:841
  316.1 22.8 %collective-permute-start.30 = (bf16[192,256]{1,0:T(8,128)(2,1)S(1)}, bf16[192,256]{1,0:T(8,128)(2,1)}, u32[]{:S(2)}, u32[]{:S(2)}) collective-permute-start(bf16[192,256]{1,0:T(8,128)(2,1)S(1)} %copy-done.38), channel_id=1, source_target_pairs={{0,2},{1,3},{2,0},{3,1},{4,6},{5,7},{6,4},{7,5},{8,10},{9,11},{10,... | collective-permute-start | bytes 294920 | tf_op jit(solution)/shard_map/ppermute | solution.py:841
  344.5 53.9 %collective-permute-start.37 = (bf16[8,336,384]{2,1,0:T(8,128)(2,1)}, bf16[8,336,384]{2,1,0:T(8,128)(2,1)}, u32[]{:S(2)}, u32[]{:S(2)}) collective-permute-start(bf16[8,336,384]{2,1,0:T(8,128)(2,1)} %pad_maximum_fusion.2), channel_id=1, source_target_pairs={{0,16},{8,24},{16,0},{24,8},{1,17},{9,25},{17,1},{25,9},{2,18},{10... | collective-permute-start | bytes 6193160 | tf_op jit(solution)/shard_map/ppermute | solution.py:753
  345.3 50.0 %collective-permute-start.34 = (bf16[2,96,2304]{2,1,0:T(8,128)(2,1)}, bf16[2,96,2304]{2,1,0:T(8,128)(2,1)}, u32[]{:S(2)}, u32[]{:S(2)}) collective-permute-start(bf16[2,96,2304]{2,1,0:T(8,128)(2,1)} %get-tuple-element.283), channel_id=1, source_target_pairs={{0,1},{1,0},{2,3},{3,2},{4,5},{5,4},{6,7},{7,6},{8,9},{9,8},{10,11... | collective-permute-start | bytes 2654216 | tf_op jit(solution)/shard_map/ppermute | solution.py:841
  346.9 48.5 %collective-permute-start.35 = (bf16[2,96,2304]{2,1,0:T(8,128)(2,1)}, bf16[2,96,2304]{2,1,0:T(8,128)(2,1)}, u32[]{:S(2)}, u32[]{:S(2)}) collective-permute-start(bf16[2,96,2304]{2,1,0:T(8,128)(2,1)} %get-tuple-element.284), channel_id=1, source_target_pairs={{0,2},{1,3},{2,0},{3,1},{4,6},{5,7},{6,4},{7,5},{8,10},{9,11},{10,... | collective-permute-start | bytes 2654216 | tf_op jit(solution)/shard_map/ppermute | solution.py:841
  348.4 47.0 %collective-permute-start.36 = (bf16[2,96,2304]{2,1,0:T(8,128)(2,1)}, bf16[2,96,2304]{2,1,0:T(8,128)(2,1)}, u32[]{:S(2)}, u32[]{:S(2)}) collective-permute-start(bf16[2,96,2304]{2,1,0:T(8,128)(2,1)} %get-tuple-element.285), channel_id=1, source_target_pairs={{0,3},{1,2},{2,1},{3,0},{4,7},{5,6},{6,5},{7,4},{8,11},{9,10},{10,... | collective-permute-start | bytes 2654216 | tf_op jit(solution)/shard_map/ppermute | solution.py:841
  350.3 54.1 %all-to-all-start.2 = ((bf16[4,2,336,384]{3,2,1,0:T(8,128)(2,1)}), bf16[4,2,336,384]{3,2,1,0:T(8,128)(2,1)}, u32[]{:S(2)}, u32[]{:S(2)}) async-start(bf16[4,2,336,384]{3,2,1,0:T(8,128)(2,1)} %copy.38), calls=%async_computation.2 | async-start | bytes 4128768 | tf_op jit(solution)/shard_map/all_to_all | solution.py:834
  407.3 38.9 %collective-permute-start.42 = (bf16[1,768,384]{2,1,0:T(8,128)(2,1)}, bf16[1,768,384]{2,1,0:T(8,128)(2,1)}, u32[]{:S(2)}, u32[]{:S(2)}) collective-permute-start(bf16[1,768,384]{2,1,0:T(8,128)(2,1)} %constant_dynamic-slice_fusion.1), channel_id=1, source_target_pairs={{0,4},{1,5},{2,6},{3,7},{4,0},{5,1},{6,2},{7,3},{8,12},{9,13},{10,... | collective-permute-start | bytes 1769480 | tf_op jit(solution)/shard_map/ppermute | solution.py:753
  414.9 28.8 %collective-permute-start.41 = (bf16[2,336,384]{2,1,0:T(8,128)(2,1)}, bf16[2,336,384]{2,1,0:T(8,128)(2,1)}, u32[]{:S(2)}, u32[]{:S(2)}) collective-permute-start(bf16[2,336,384]{2,1,0:T(8,128)(2,1)} %get-tuple-element.316), channel_id=1, source_target_pairs={{0,3},{1,2},{2,1},{3,0},{4,7},{5,6},{6,5},{7,4},{8,11},{9,10},{10,... | collective-permute-start | bytes 1548296 | tf_op jit(solution)/shard_map/ppermute | solution.py:841
  421.2 26.9 %all-to-all-start.3 = ((bf16[4,8,24,576]{3,2,1,0:T(8,128)(2,1)}), bf16[4,8,24,576]{3,2,1,0:T(8,128)(2,1)S(1)}, u32[]{:S(2)}, u32[]{:S(2)}) async-start(bf16[4,8,24,576]{3,2,1,0:T(8,128)(2,1)} %qkv_grad.3), calls=%async_computation.3 | async-start | bytes 1966080 | tf_op jit(solution)/shard_map/all_to_all | solution.py:957
  452.5 67.1 %all-gather.3.cloned.1.call-start = ((), (), s32[]{:S(2)}) async-start(), calls=%async_computation.6 | async-start | bytes 2949120 | tf_op jit(solution)/shard_map/all_gather | solution.py:1014
  (86 other events, 840.9 us)
Sparse Core Ops, SparseCore 0:
  461.2 24.5 all-gather.2
